TPU v7x, 32 devices: a whole 2x2x4 slice. The times are simulated.
32 devices in a mesh: rep: 4 (over y, core), vol: 8 (over z, x).
Axes of the slice: x: 2, y: 2, z: 4, core: 2. Of those that a mesh axis runs over, the one named last changes fastest.
Arguments:
- positions: float32 [8192, 2, 24], P(('rep', 'vol')), may hold values from -1 to 1
- spacing: float32 [8192, 2, 8], P(('rep', 'vol')), may hold values from 0.05 to 0.5
- volume_ids: int32 [8192, 2], P(('rep', 'vol')), may hold values from 0 to 31, all different within a row; in each aligned block of 256 rows (0 to 255, 256 to 511, ...) at most 32 rows name the same one
- target: float32 [3, 8192], P(None, ('rep', 'vol')), may hold values from 0 to 1
- w_in: bfloat16 [32, 64, 256], P('vol'), may hold values from -0.75 to 0.75
- w_hidden: bfloat16 [32, 256, 256], P('vol'), may hold values from -0.375 to 0.375
- w_head: bfloat16 [32, 4, 256], P('vol'), may hold values from -0.375 to 0.375
Outputs:
- rendered: float32 [3, 8192], P(None, ('rep', 'vol'))
- grad_in: float32 [32, 64, 256], P('vol', None, 'rep')
- grad_hidden: float32 [32, 256, 256], P('vol', 'rep')
- grad_head: float32 [32, 4, 256], P('vol', None, 'rep')
Inputs may be any that keep to these rules, and one draw needn't show every extreme that they name: `volume_ids`: the 2 entries of a ray are different sub-volumes, nearest first. Among the 256 rays of one device no sub-volume is named more than 32 times, and in some device's rays one is named exactly 32 times.
All inputs are finite; a program needn't handle non-finite values.
Results may differ from a plain program's by a relative error of at most 0.012.
Values may be sent and summed in bfloat16 or wider, within the bound.
No kernel may reach another device: no remote copies, remote signals or barrier semaphores. Data moves between devices by JAX's collectives and lax.ppermute only.
A program may use at most 64 MiB of HBM per device.

v0:
```python
import math

import jax
import jax.numpy as jnp
from jax import lax
from jax.sharding import PartitionSpec as P

FREQS = 10
ENC = 64


def encode(points):
    coords = jnp.swapaxes(points, -1, -2)
    scales = (2.0 ** jnp.arange(FREQS)).astype(jnp.float32) * math.pi
    angles = (coords[..., None] * scales).reshape(coords.shape[:-1] + (3 * FREQS,))
    unit = jnp.ones(coords.shape[:-1] + (1,), jnp.float32)
    return jnp.concatenate([jnp.sin(angles), jnp.cos(angles), coords, unit], axis=-1)


def silu_slope(pre_act):
    gate = jax.nn.sigmoid(pre_act)
    return gate * (1.0 + pre_act * (1.0 - gate))


def product(left, right):
    return jnp.dot(left, right, preferred_element_type=jnp.float32)


def forward(rows, w_first, w_mid, w_last):
    pre_one = product(rows, w_first)
    act_one = jax.nn.silu(pre_one).astype(jnp.bfloat16)
    pre_two = product(act_one, w_mid)
    act_two = jax.nn.silu(pre_two).astype(jnp.bfloat16)
    raw_out = product(act_two, w_last.T)
    return (pre_one, act_one, pre_two, act_two, raw_out)


def activate(raw_out):
    return jnp.concatenate(
        [jax.nn.sigmoid(raw_out[:, :3]), jax.nn.softplus(raw_out[:, 3:])], axis=1
    )


def backward(rows, cotangent, w_first, w_mid, w_last):
    pre_one, act_one, pre_two, act_two, raw_out = forward(rows, w_first, w_mid, w_last)
    gate = jax.nn.sigmoid(raw_out)
    slope = jnp.concatenate([gate[:, :3] * (1.0 - gate[:, :3]), gate[:, 3:]], axis=1)
    cot_raw = (cotangent * slope).astype(jnp.bfloat16)
    d_last = product(cot_raw.T, act_two)
    cot_two = (product(cot_raw, w_last) * silu_slope(pre_two)).astype(jnp.bfloat16)
    d_mid = product(act_one.T, cot_two)
    cot_one = (product(cot_two, w_mid.T) * silu_slope(pre_one)).astype(jnp.bfloat16)
    d_first = product(rows.T, cot_one)
    return (d_first, d_mid, d_last)


def slots_of(volume_ids, volume_count, capacity):
    flat_ids = volume_ids.reshape(-1)
    table = (flat_ids[:, None] == jnp.arange(volume_count, dtype=jnp.int32)[None, :]).astype(
        jnp.int32
    )
    earlier = jnp.cumsum(table, axis=0) - table
    return flat_ids * capacity + jnp.sum(earlier * table, axis=1)


def segment_values(radiance, spacing):
    tau = radiance[..., 3] * spacing
    alpha = 1.0 - jnp.exp(-tau)
    before = jnp.cumsum(tau, axis=-1) - tau
    share = jnp.exp(-before) * alpha
    seg_color = jnp.sum(share[..., None] * radiance[..., :3], axis=-2)
    passing = jnp.exp(-jnp.sum(tau, axis=-1))
    return jnp.concatenate([seg_color, passing[..., None]], axis=-1)


def combine(per_seg):
    color = per_seg[:, 0, :3]
    carried = per_seg[:, 0, 3]
    color = color + carried[:, None] * per_seg[:, 1, :3]
    return color.T


def local(positions, spacing, volume_ids, target, w_in, w_hidden, w_head):
    ray_count, seg_count = volume_ids.shape
    sample_count = spacing.shape[2]
    owners = lax.axis_size("vol")
    held_count = w_in.shape[0]
    volume_count = owners * held_count
    capacity = 2 * ray_count * seg_count // volume_count
    row_count = owners * capacity * sample_count
    places = slots_of(volume_ids, volume_count, capacity)
    gap_slots = (
        jnp.zeros((volume_count * capacity, sample_count), jnp.float32)
        .at[places]
        .set(spacing.reshape(ray_count * seg_count, sample_count))
    )
    gap_slots = gap_slots.reshape(owners, held_count * capacity, sample_count)
    points = positions.reshape(ray_count * seg_count, 3, sample_count)
    feats = encode(points).astype(jnp.bfloat16).reshape(ray_count * seg_count, sample_count * ENC)
    outgoing = (
        jnp.zeros((volume_count * capacity, sample_count * ENC), jnp.bfloat16).at[places].set(feats)
    )
    outgoing = outgoing.reshape(owners, held_count * capacity, sample_count * ENC)
    arrived, gap_arrived = (
        lax.all_to_all(outgoing, "vol", split_axis=0, concat_axis=0, tiled=True),
        lax.all_to_all(
            gap_slots.astype(jnp.bfloat16), "vol", split_axis=0, concat_axis=0, tiled=True
        ).astype(gap_slots.dtype),
    )
    features = arrived.reshape(owners, held_count, capacity * sample_count, ENC)
    rows = jnp.swapaxes(features, 0, 1).reshape(held_count, row_count, ENC)
    radiance = lax.map(lambda item: activate(forward(*item)[4]), (rows, w_in, w_hidden, w_head))
    gaps_here = jnp.swapaxes(gap_arrived.reshape(owners, held_count, capacity, sample_count), 0, 1)
    samples_here = radiance.reshape(held_count, owners, capacity, sample_count, 4)
    seg_here, seg_pull = jax.vjp(lambda values: segment_values(values, gaps_here), samples_here)
    leaving = jnp.swapaxes(seg_here, 0, 1).reshape(owners, held_count * capacity, 4)
    returned = lax.all_to_all(leaving, "vol", split_axis=0, concat_axis=0, tiled=True)
    per_seg = returned.reshape(volume_count * capacity, 4)[places].reshape(ray_count, seg_count, 4)
    color, pull = jax.vjp(combine, per_seg)
    (cot_seg,) = pull((color - target) / lax.axis_size("rep"))
    cot_out = (
        jnp.zeros((volume_count * capacity, 4), jnp.float32)
        .at[places]
        .set(cot_seg.reshape(ray_count * seg_count, 4))
    )
    cot_back = lax.all_to_all(
        cot_out.reshape(owners, held_count * capacity, 4),
        "vol",
        split_axis=0,
        concat_axis=0,
        tiled=True,
    )
    cot_here = jnp.swapaxes(cot_back.reshape(owners, held_count, capacity, 4), 0, 1)
    (cot_samples,) = seg_pull(cot_here)
    cot_rows = cot_samples.reshape(held_count, row_count, 4)
    partial_grads = lax.map(lambda item: backward(*item), (rows, cot_rows, w_in, w_hidden, w_head))
    grad_in, grad_hidden, grad_head = (
        lax.psum_scatter(partial_grads[0], "rep", scatter_dimension=2, tiled=True),
        lax.psum_scatter(partial_grads[1], "rep", scatter_dimension=1, tiled=True),
        lax.psum_scatter(partial_grads[2], "rep", scatter_dimension=2, tiled=True),
    )
    return (color, grad_in, grad_hidden, grad_head)


def solution(mesh):
    return jax.shard_map(
        local,
        mesh=mesh,
        in_specs=(
            P(("rep", "vol"), None, None),
            P(("rep", "vol"), None, None),
            P(("rep", "vol"), None),
            P(None, ("rep", "vol")),
            P("vol", None, None),
            P("vol", None, None),
            P("vol", None, None),
        ),
        out_specs=(
            P(None, ("rep", "vol")),
            P("vol", None, "rep"),
            P("vol", "rep", None),
            P("vol", None, "rep"),
        ),
        check_vma=False,
    )
```

profile of v0, /device:TPU:1, one launch (start us, length us, event | category | flops | bytes accessed | tf_op | source)
XLA Modules:
  0.0 237.5 jit_solution(16489333903105260679)
XLA Ops:
  14.3 6.4 %all-to-all-start.1 = ((bf16[8,128,8]{1,2,0:T(8,128)(2,1)}), bf16[8,128,8]{1,2,0:T(8,128)(2,1)S(1)}, u32[]{:S(2)}, u32[]{:S(2)}) async-start(bf16[8,128,8]{1,2,0:T(8,128)(2,1)} %bitcast.170), calls=%async_computation.1 | async-start | bytes 32768 | tf_op jit(solution)/shard_map/all_to_all | solution.py:106
  24.1 3.5 %scatter_custom_fusion = bf16[1024,512]{1,0:T(8,128)(2,1)} fusion(s32[512]{0:T(512)S(1)} %bitcast.246, bf16[512,512]{1,0:T(8,128)(2,1)S(1)} %copy.114, bf16[]{:T(256)} %constant.59.clone.1), kind=kCustom, calls=%fused_computation.89 | custom fusion | bytes 1048578 | tf_op jit(solution)/shard_map/scatter | solution.py:101
  27.6 5.4 %all-to-all-start = ((bf16[8,128,512]{2,1,0:T(8,128)(2,1)}), bf16[8,128,512]{2,1,0:T(8,128)(2,1)S(1)}, u32[]{:S(2)}, u32[]{:S(2)}) async-start(bf16[8,128,512]{2,1,0:T(8,128)(2,1)} %bitcast.22), calls=%async_computation | async-start | bytes 2097152 | tf_op jit(solution)/shard_map/all_to_all | solution.py:105
  34.2 23.3 %all-to-all-done = bf16[8,128,512]{2,1,0:T(8,128)(2,1)S(1)} async-done(((bf16[8,128,512]{2,1,0:T(8,128)(2,1)}), bf16[8,128,512]{2,1,0:T(8,128)(2,1)S(1)}, u32[]{:S(2)}, u32[]{:S(2)}) %all-to-all-start) | async-done | bytes 1048608 | tf_op jit(solution)/shard_map/all_to_all | solution.py:105
  61.4 13.4 %while.24 = (s32[]{:T(128)}, f32[4,2048,4]{1,2,0:T(4,128)S(1)}, bf16[4,2048,64]{2,1,0:T(8,128)(2,1)S(1)}, bf16[4,64,256]{2,1,0:T(8,128)(2,1)S(1)}, bf16[4,256,25...) while((s32[]{:T(128)}, f32[4,2048,4]{1,2,0:T(4,128)S(1)}, bf16[4,2048,64]{2,1,0:T(8,128)(2,1)S(1)}, ...), condition=%wide.region_5.6_spmd, body=%wide.region_4.5_spmd.sunk | while | flops 345020416 | bytes 2961489 | solution.py:112
  61.5 2.1 multiply_convert_fusion.9
  64.8 2.1 multiply_convert_fusion.9
  68.2 2.1 multiply_convert_fusion.9
  71.5 2.1 multiply_convert_fusion.9
  77.6 5.3 %reduce_window_sum.39 = f32[4,8,32,8]{3,2,1,0:T(8,128)S(1)} reduce-window(f32[4,8,32,8]{3,2,1,0:T(8,128)S(1)} %get-tuple-element.182, f32[]{:T(128)} %constant.53.clone.1), window={size=1x1x1x8 pad=0_0x0_0x0_0x7_0}, to_apply=%region_7.8 | reduce-window | flops 57344 | bytes 65540 | tf_op jit(solution)/shard_map/jvp(jit(cumsum))/reduce_window_sum | solution.py:69
  86.2 5.1 %all-to-all-start.2 = ((f32[8,128,4]{1,2,0:T(4,128)}), f32[8,128,4]{1,2,0:T(4,128)S(1)}, u32[]{:S(2)}, u32[]{:S(2)}) async-start(f32[8,128,4]{1,2,0:T(4,128)} %reshape.145), calls=%async_computation.2 | async-start | bytes 32768 | tf_op jit(solution)/shard_map/all_to_all | solution.py:117
  91.9 4.8 %all-to-all-done.2 = f32[8,128,4]{1,2,0:T(4,128)S(1)} async-done(((f32[8,128,4]{1,2,0:T(4,128)}), f32[8,128,4]{1,2,0:T(4,128)S(1)}, u32[]{:S(2)}, u32[]{:S(2)}) %all-to-all-start.2) | async-done | bytes 16416 | tf_op jit(solution)/shard_map/all_to_all | solution.py:117
  104.0 3.3 %all-to-all-start.3 = ((f32[8,128,4]{1,2,0:T(4,128)}), f32[8,128,4]{1,2,0:T(4,128)S(1)}, u32[]{:S(2)}, u32[]{:S(2)}) async-start(f32[8,128,4]{1,2,0:T(4,128)} %copy.128), calls=%async_computation.3 | async-start | bytes 32768 | tf_op jit(solution)/shard_map/all_to_all | solution.py:126
  107.6 5.1 %all-to-all-done.3 = f32[8,128,4]{1,2,0:T(4,128)S(1)} async-done(((f32[8,128,4]{1,2,0:T(4,128)}), f32[8,128,4]{1,2,0:T(4,128)S(1)}, u32[]{:S(2)}, u32[]{:S(2)}) %all-to-all-start.3) | async-done | bytes 16416 | tf_op jit(solution)/shard_map/all_to_all | solution.py:126
  113.5 3.6 %broadcast_multiply_fusion = (f32[4,8,32,8,3]{3,2,1,4,0:T(8,128)}, f32[4,8,32,8]{3,2,1,0:T(8,128)}) fusion(f32[4,8,32,8]{3,2,1,0:T(8,128)} %subtract_multiply_fusion.1, f32[4,8,32,8,4]{3,2,1,4,0:T(8,128)S(1)} %reshape.142, f32[4,8,32,4]{2,1,0,3:T(8,128)S(1)} %bitcast.242), kind=kLoop, calls=%fused_computation.80 | loop fusion | flops 65536 | bytes 1785856 | tf_op jit(solution)/shard_map/transpose(jvp())/mul | solution.py:71
  118.4 5.3 %reduce_window_sum.40 = f32[4,8,32,8]{3,2,1,0:T(8,128)S(1)} reduce-window(f32[4,8,32,8]{3,2,1,0:T(8,128)S(1)} %fusion.70, f32[]{:T(128)} %constant.53.clone.1), window={size=1x1x1x8 pad=0_0x0_0x0_0x0_7}, to_apply=%region_13.14 | reduce-window | flops 57344 | bytes 65540 | tf_op jit(solution)/shard_map/transpose(jvp(jit(cumsum)))/reduce_window_sum | solution.py:69
  126.7 32.9 %while.25 = (s32[]{:T(128)}, f32[4,64,256]{2,1,0:T(8,128)S(1)}, f32[4,256,256]{2,1,0:T(8,128)}, f32[4,4,256]{2,1,0:T(4,128)S(1)}, bf16[4,2048,64]{2,1,0:T(8,128)...) while((s32[]{:T(128)}, f32[4,64,256]{2,1,0:T(8,128)S(1)}, ...), condition=%wide.region_15.16_spmd, body=%wide.region_14.15_spmd.sunk | while | flops 969494528 | bytes 25031816 | solution.py:136
  132.4 2.5 %fusion.154 = f32[4,64,256]{2,1,0:T(8,128)S(1)} fusion(f32[4,64,256]{2,1,0:T(8,128)S(1)} %get-tuple-element.331, s32[]{:T(128)} %get-tuple-element.330, bf16[2048,256]{1,0:T(8,128)(2,1)} %copy-done.14, f32[2048,256]{1,0:T(8,128)S(1)} %fusion.150, bf16[4,2048,64]{2,1,0:T(8,128)(2,1)} %get-tuple-element.344, ...), kind=kOutput, calls=%fused_computation.43.clone.1 | convolution fusion | flops 340262912 | bytes 3868160 | tf_op jit(solution)/shard_map/while/body/eval_jaxpr/dot_general | solution.py:26
  140.6 2.5 %fusion.154 = f32[4,64,256]{2,1,0:T(8,128)S(1)} fusion(f32[4,64,256]{2,1,0:T(8,128)S(1)} %get-tuple-element.331, s32[]{:T(128)} %get-tuple-element.330, bf16[2048,256]{1,0:T(8,128)(2,1)} %copy-done.14, f32[2048,256]{1,0:T(8,128)S(1)} %fusion.150, bf16[4,2048,64]{2,1,0:T(8,128)(2,1)} %get-tuple-element.344, ...), kind=kOutput, calls=%fused_computation.43.clone.1 | convolution fusion | flops 340262912 | bytes 3868160 | tf_op jit(solution)/shard_map/while/body/eval_jaxpr/dot_general | solution.py:26
  148.9 2.5 %fusion.154 = f32[4,64,256]{2,1,0:T(8,128)S(1)} fusion(f32[4,64,256]{2,1,0:T(8,128)S(1)} %get-tuple-element.331, s32[]{:T(128)} %get-tuple-element.330, bf16[2048,256]{1,0:T(8,128)(2,1)} %copy-done.14, f32[2048,256]{1,0:T(8,128)S(1)} %fusion.150, bf16[4,2048,64]{2,1,0:T(8,128)(2,1)} %get-tuple-element.344, ...), kind=kOutput, calls=%fused_computation.43.clone.1 | convolution fusion | flops 340262912 | bytes 3868160 | tf_op jit(solution)/shard_map/while/body/eval_jaxpr/dot_general | solution.py:26
  157.1 2.5 %fusion.154 = f32[4,64,256]{2,1,0:T(8,128)S(1)} fusion(f32[4,64,256]{2,1,0:T(8,128)S(1)} %get-tuple-element.331, s32[]{:T(128)} %get-tuple-element.330, bf16[2048,256]{1,0:T(8,128)(2,1)} %copy-done.14, f32[2048,256]{1,0:T(8,128)S(1)} %fusion.150, bf16[4,2048,64]{2,1,0:T(8,128)(2,1)} %get-tuple-element.344, ...), kind=kOutput, calls=%fused_computation.43.clone.1 | convolution fusion | flops 340262912 | bytes 3868160 | tf_op jit(solution)/shard_map/while/body/eval_jaxpr/dot_general | solution.py:26
  162.9 16.9 %reduce-scatter.12.cloned.1.call-done = f32[64,16]{1,0:T(8,128)} async-done(((f32[256,16]{1,0:T(8,128)}), f32[64,16]{1,0:T(8,128)}) %reduce-scatter.12.cloned.1.call-update) | async-done | bytes 4112
  181.3 21.5 %reduce-scatter.10.cloned.1.call-done = f32[64,256]{1,0:T(8,128)} async-done(((f32[256,256]{1,0:T(8,128)}), f32[64,256]{1,0:T(8,128)}) %reduce-scatter.10.cloned.1.call-update) | async-done | bytes 65552
  204.6 26.4 %reduce-scatter.8.cloned.1.call-done = f32[4,64,256]{2,1,0:T(8,128)} async-done(((f32[4,256,256]{2,1,0:T(8,128)}), f32[4,64,256]{2,1,0:T(8,128)}) %reduce-scatter.8.cloned.1.call-update) | async-done | bytes 262160 | tf_op jit(solution)/shard_map/reduce_scatter | solution.py:139
  (165 shorter events, 68.5 us)
Async XLA Ops:
  7.2 13.5 %copy-start.9 = (f32[256,2,24]{0,2,1:T(8,128)S(1)}, f32[256,2,24]{0,2,1:T(8,128)}, u32[]{:S(2)}) copy-start(f32[256,2,24]{0,2,1:T(8,128)} %param.11) | copy-start | bytes 147460
  11.7 79.6 %copy-start.12 = (s32[512,1]{0,1:T(1,128)}, s32[512,1]{0,1:T(1,128)S(1)}, u32[]{:S(2)}) copy-start(s32[512,1]{0,1:T(1,128)S(1)} %compare_select_fusion.1) | copy-start | bytes 6148
  14.3 13.3 %all-to-all-start.1 = ((bf16[8,128,8]{1,2,0:T(8,128)(2,1)}), bf16[8,128,8]{1,2,0:T(8,128)(2,1)S(1)}, u32[]{:S(2)}, u32[]{:S(2)}) async-start(bf16[8,128,8]{1,2,0:T(8,128)(2,1)} %bitcast.170), calls=%async_computation.1 | async-start | bytes 32768 | tf_op jit(solution)/shard_map/all_to_all | solution.py:106
  27.6 29.9 %all-to-all-start = ((bf16[8,128,512]{2,1,0:T(8,128)(2,1)}), bf16[8,128,512]{2,1,0:T(8,128)(2,1)S(1)}, u32[]{:S(2)}, u32[]{:S(2)}) async-start(bf16[8,128,512]{2,1,0:T(8,128)(2,1)} %bitcast.22), calls=%async_computation | async-start | bytes 2097152 | tf_op jit(solution)/shard_map/all_to_all | solution.py:105
  59.7 1.8 copy-start.6
  74.9 1.4 copy-start
  82.9 9.0 %copy-start.1 = (f32[4,8,32,8]{3,2,1,0:T(8,128)}, f32[4,8,32,8]{3,2,1,0:T(8,128)S(1)}, u32[]{:S(2)}) copy-start(f32[4,8,32,8]{3,2,1,0:T(8,128)S(1)} %reduce_window_sum.39) | copy-start | bytes 98308
  86.2 10.5 %all-to-all-start.2 = ((f32[8,128,4]{1,2,0:T(4,128)}), f32[8,128,4]{1,2,0:T(4,128)S(1)}, u32[]{:S(2)}, u32[]{:S(2)}) async-start(f32[8,128,4]{1,2,0:T(4,128)} %reshape.145), calls=%async_computation.2 | async-start | bytes 32768 | tf_op jit(solution)/shard_map/all_to_all | solution.py:117
  99.6 1.6 copy-start.10
  104.0 8.7 %all-to-all-start.3 = ((f32[8,128,4]{1,2,0:T(4,128)}), f32[8,128,4]{1,2,0:T(4,128)S(1)}, u32[]{:S(2)}, u32[]{:S(2)}) async-start(f32[8,128,4]{1,2,0:T(4,128)} %copy.128), calls=%async_computation.3 | async-start | bytes 32768 | tf_op jit(solution)/shard_map/all_to_all | solution.py:126
  107.3 72.4 %reduce-scatter.12.cloned.1.call-start = ((), (), s32[]{:S(2)}) async-start(), calls=%async_computation.9 | async-start | bytes 163840
  113.5 3.6 %copy-start.2 = (f32[4,8,32,8]{3,2,1,0:T(8,128)S(1)}, f32[4,8,32,8]{3,2,1,0:T(8,128)}, u32[]{:S(2)}) copy-start(f32[4,8,32,8]{3,2,1,0:T(8,128)} %copy-done.1) | copy-start | bytes 98308
  117.1 6.6 %copy-start.5 = (f32[8,4,32,8]{3,2,0,1:T(8,128)S(1)}, f32[8,4,32,8]{3,2,0,1:T(8,128)}, u32[]{:S(2)}) copy-start(f32[8,4,32,8]{3,2,0,1:T(8,128)} %copy.120) | copy-start | bytes 98308
  117.1 6.6 %copy-start.7 = (f32[4,8,32]{2,1,0:T(8,128)S(1)}, f32[4,8,32]{2,1,0:T(8,128)}, u32[]{:S(2)}) copy-start(f32[4,8,32]{2,1,0:T(8,128)} %fusion.84) | copy-start | bytes 12292
  123.7 1.6 copy-start.3
  125.5 1.1 copy-start.8
  125.5 1.1 copy-start.11
  125.5 1.1 copy-start.13
  131.0 1.5 copy-start.14
  139.2 1.5 copy-start.14
  147.4 1.4 copy-start.14
  155.6 1.5 copy-start.14
  160.8 42.1 %reduce-scatter.10.cloned.1.call-start = ((), (), s32[]{:S(2)}) async-start(), calls=%async_computation.8 | async-start | bytes 327680
  162.1 68.8 %reduce-scatter.8.cloned.1.call-start = ((), (), s32[]{:S(2)}) async-start(), calls=%async_computation.7 | async-start | bytes 1310720 | tf_op jit(solution)/shard_map/reduce_scatter | solution.py:139
  (1 other events, 1.1 us)
Sparse Core Ops, SparseCore 0:
  160.9 18.7 reduce-scatter.11
  182.3 20.4 reduce-scatter.9
  206.0 24.9 reduce-scatter.7
where the time goes:
time: 239 us; the launch traced here: 237 us
  waiting for transfers between devices  98.7 us (41%)
  matrix products  45.2 us (19%)
  local copies, waits for them, and re-layouts  30.5 us (13%)
  other arithmetic  27.9 us (12%)
  starting transfers between devices  20.5 us (9%)
  between operations  14.2 us (6%)
    dot_general x36, matrix products, product(): return jnp.dot(left, right, preferred_element_type=jnp.float32)  45.2 us
    unnamed x5, waiting for transfers between devices  39.1 us
    reduce_scatter x1, waiting for transfers between devices, local(): lax.psum_scatter(partial_grads[1], 'rep', scatter_dimension=1, tiled=True)  26.4 us
    all_to_all x1, waiting for transfers between devices, local(): lax.all_to_all(outgoing, 'vol', split_axis=0, concat_axis=0, tiled=True)  23.3 us
    another operation x2, other arithmetic, segment_values(): before = jnp.cumsum(tau, axis=-1) - tau  10.6 us
    unnamed x42, local copies, waits for them, and re-layouts  9.27 us
    all_to_all x1, starting transfers between devices, local(): lax.all_to_all(gap_slots.astype(jnp.bfloat16), 'vol', split_axis=0, conca...  6.35 us
    all_to_all x1, starting transfers between devices, local(): lax.all_to_all(outgoing, 'vol', split_axis=0, concat_axis=0, tiled=True)  5.43 us
  transfers between devices with their start and end apart: 7, of which 6 were waited for; matrix products, arithmetic and copies ran while one was open for 6% of the time, Pallas kernels for 0%

commit v1 on v0

v1 whole, which is shorter than its diff:
```python
import functools

import jax
import jax.numpy as jnp
from jax import lax
from jax.experimental import pallas as pl
from jax.experimental.pallas import tpu as pltpu
from jax.sharding import PartitionSpec as P

FREQS = 10
COORDS = 3
CHUNK = 4
FORWARD_CHUNK = 2
PAYLOAD = 40
BF = jnp.bfloat16
F32 = jnp.float32

COS_PI = (
    0.9999999889445765,
    -4.9348011166440395,
    4.058694745521683,
    -1.3351580223048074,
    0.23502902262478848,
    -0.025358285754444,
    0.0015936782135993002,
)
COS_TURN = tuple(factor * 4.0**power for power, factor in enumerate(COS_PI))
ROUNDER = 12582912.0

NT = (((1,), (1,)), ((), ()))
TN = (((0,), (0,)), ((), ()))


def mm(left, right):
    return jnp.dot(left, right, preferred_element_type=F32)


def mm_nt(left, right):
    return lax.dot_general(left, right, NT, preferred_element_type=F32)


def split3(values):
    high = values.astype(BF).astype(F32)
    rest = values - high
    middle = rest.astype(BF).astype(F32)
    low = rest - middle
    return jnp.concatenate([high, middle, low], axis=0).astype(BF)


def join3(stacked, count):
    return stacked[:count] + stacked[count : 2 * count] + stacked[2 * count :]


def one_hot_rows(count, row):
    shape = (count, row.shape[1])
    same = lax.broadcasted_iota(jnp.int32, shape, 0) == row
    return jnp.where(same, 1.0, 0.0).astype(BF)


def sigmoid(value):
    return 0.5 + 0.5 * jnp.tanh(0.5 * value)


def softplus(value):
    return jnp.maximum(value, 0.0) + jnp.log1p(jnp.exp(-jnp.abs(value)))


def dispatch_kernel(
    volume_count,
    capacity,
    pos_hbm,
    gap_hbm,
    ids_hbm,
    tgt_hbm,
    out_hbm,
    place_hbm,
    pos_ref,
    gap_ref,
    ids_ref,
    tgt_ref,
    out_ref,
    place_ref,
    sems,
):
    copies = [
        pltpu.make_async_copy(source, target, sems.at[index])
        for index, (source, target) in enumerate(
            [(ids_hbm, ids_ref), (pos_hbm, pos_ref), (gap_hbm, gap_ref), (tgt_hbm, tgt_ref)]
        )
    ]
    for copy in copies:
        copy.start()
    rays = pos_ref.shape[2]
    segs = 2 * rays
    owners, _, width = out_ref.shape
    upper = jnp.where(
        lax.broadcasted_iota(jnp.int32, (segs, segs), 0)
        < lax.broadcasted_iota(jnp.int32, (segs, segs), 1),
        1.0,
        0.0,
    ).astype(BF)
    copies[0].wait()
    ids = jnp.concatenate([ids_ref[0:1, :], ids_ref[1:2, :]], axis=1)
    same = lax.broadcasted_iota(jnp.int32, (volume_count, segs), 0) == ids
    table = jnp.where(same, 1.0, 0.0)
    earlier = mm(table.astype(BF), upper)
    rank = jnp.sum(earlier * table, axis=0, keepdims=True)
    place = ids * capacity + rank.astype(jnp.int32)
    place_ref[...] = place
    place_f = place.astype(F32)
    partner = jnp.concatenate([place_f[:, rays:], place_f[:, :rays]], axis=1)
    second = jnp.where(lax.broadcasted_iota(jnp.int32, (1, segs), 1) >= rays, 1.0, 0.0)
    for copy in copies[1:]:
        copy.wait()
    tgt = tgt_ref[...]
    extra = jnp.concatenate(
        [jnp.concatenate([tgt, tgt], axis=1), partner, second, jnp.zeros((3, segs), F32)], axis=0
    )
    values = jnp.concatenate(
        [
            jnp.concatenate([pos_ref[0], pos_ref[1]], axis=1),
            jnp.concatenate([gap_ref[0], gap_ref[1]], axis=1),
            extra,
        ],
        axis=0,
    )
    writes = [pltpu.make_async_copy(place_ref, place_hbm, sems.at[4])]
    writes[0].start()
    pieces = split3(values)
    half = owners // 2
    for part in range(2):
        hot = one_hot_rows(half * width, place - part * half * width)
        slots = join3(mm_nt(pieces, hot), PAYLOAD)
        for n in range(half):
            out_ref[part * half + n] = slots[:, n * width : (n + 1) * width]
        block = pl.ds(part * half, half)
        writes.append(
            pltpu.make_async_copy(out_ref.at[block], out_hbm.at[block], sems.at[5 + part])
        )
        writes[-1].start()
    for write in writes:
        write.wait()


def selection(samples, start):
    shape = (128, samples * 64)
    source = lax.broadcasted_iota(jnp.int32, shape, 0) + start
    column = lax.broadcasted_iota(jnp.int32, shape, 1)
    sample, entry = column // 64, column % 64
    angle = jnp.where(entry < 30, entry, entry - 30)
    axis = jnp.where(entry < 60, angle // FREQS, entry - 60)
    power = jnp.where(entry < 60, angle % FREQS, 1)
    factor = 0.5 * lax.shift_left(jnp.ones(shape, jnp.int32), power).astype(F32)
    wanted = (source < 72) & (source % 24 == axis * samples + sample) & (entry < 63)
    constant = jnp.where(entry < 30, -0.25, jnp.where(entry == 63, 1.0, 0.0))
    value = jnp.where(wanted, factor, jnp.where(source == 72, constant, 0.0))
    return value.astype(BF)


def wave(turns):
    turns = turns - ((turns + ROUNDER) - ROUNDER)
    square = turns * turns
    value = square * COS_TURN[-1] + COS_TURN[-2]
    for factor in COS_TURN[-3::-1]:
        value = value * square + factor
    return value


def silu(half):
    half = half.astype(BF)
    up = jnp.asarray(1.0, BF) + jnp.tanh(half)
    return half * up, up


def segment_parts(half_raw, gaps):
    samples = gaps.shape[1]
    gates = [
        0.5 + 0.5 * jnp.tanh(half_raw[:, c * samples : (c + 1) * samples]) for c in range(4)
    ]
    tau = softplus(2.0 * half_raw[:, 3 * samples :]) * gaps
    before = [jnp.zeros_like(tau[:, :1])]
    for sample in range(1, samples + 1):
        before.append(before[-1] + tau[:, sample - 1 : sample])
    ahead = jnp.exp(-jnp.concatenate(before[:-1], axis=1))
    thinned = jnp.exp(-tau)
    share = ahead * (1.0 - thinned)
    return gates, ahead, thinned, share, jnp.exp(-before[-1])


def forward_kernel(
    capacity,
    in_ref,
    picks_ref,
    pair_ref,
    w2_ref,
    w3_ref,
    slots_ref,
    enc_t_ref,
    seg_ref,
    send_ref,
    terms_ref,
    *rest,
):
    stored, raw_ref = rest[:-1], rest[-1]
    owners = in_ref.shape[0]
    held, hidden, _ = w2_ref.shape
    features = pair_ref.shape[1] // 2
    samples = 8
    width = owners * capacity
    for vol in range(held):
        for src in range(owners):
            slots_ref[vol, :, src * capacity : (src + 1) * capacity] = in_ref[
                src, :, vol * capacity : (vol + 1) * capacity
            ]
    plain = lax.broadcasted_iota(jnp.int32, (1, samples * features), 1) % features >= 60

    def encode(vol):
        pieces = split3(slots_ref[vol, 0:24, :]).astype(F32)
        points = jnp.concatenate(
            [pieces, jnp.ones((8, width), F32), jnp.zeros((48, width), F32)], axis=0
        )
        turns = mm(points.T.astype(BF), picks_ref[...])
        return jnp.where(plain, turns, wave(turns)).astype(BF)

    def first(enc, i, pair):
        pairs = [enc[:, j * features : (j + 2) * features] for j in range(i, i + FORWARD_CHUNK, 2)]
        both = mm(jnp.concatenate(pairs, axis=0), pair)
        return jnp.concatenate(
            [
                both[n * width : (n + 1) * width, j * hidden : (j + 1) * hidden]
                for n in range(FORWARD_CHUNK // 2)
                for j in range(2)
            ],
            axis=0,
        )

    order = [(vol, i) for vol in range(held) for i in range(0, samples, FORWARD_CHUNK)]
    enc, half_one, act_one, half_two = {0: encode(0)}, {}, {}, {}
    for step in range(len(order) + 3):
        stores = []
        if step < len(order):
            vol, i = order[step]
            half_one[step] = first(enc[vol], i, pair_ref[vol])
            if i == 0 and vol + 1 < held:
                enc[vol + 1] = encode(vol + 1)
            turned = enc[vol][:, i * features : (i + FORWARD_CHUNK) * features].T
            for j in range(FORWARD_CHUNK):
                lanes = pl.ds((i + j) * width, width)
                stores.append(
                    (enc_t_ref.at[vol, :, lanes], turned[j * features : (j + 1) * features])
                )
        at = step - 2
        if 0 <= at < len(order):
            half_two[at] = mm(act_one.pop(at), w2_ref[order[at][0]])
        at = step - 1
        if 0 <= at < len(order):
            vol, i = order[at]
            act_one[at], up = silu(half_one.pop(at))
            rows = pl.ds(i * width, FORWARD_CHUNK * width)
            stores.append((stored[4 * vol].at[rows, :], act_one[at]))
            stores.append((stored[4 * vol + 2].at[rows, :], up))
        at = step - 3
        if 0 <= at < len(order):
            vol, i = order[at]
            act_two, up = silu(half_two.pop(at))
            rows = pl.ds(i * width, FORWARD_CHUNK * width)
            stores.append((stored[4 * vol + 1].at[rows, :], act_two))
            stores.append((stored[4 * vol + 3].at[rows, :], up))
            values = mm(act_two, w3_ref[vol])
            for j in range(FORWARD_CHUNK):
                part = values[j * width : (j + 1) * width]
                raw = part if i + j == 0 else raw + pltpu.roll(part, i + j, 1)
            if i + FORWARD_CHUNK == samples:
                stores.append((raw_ref.at[vol], raw.T[: 4 * samples]))
        for ref, value in stores:
            ref[...] = value

    gaps = slots_ref[:, 24:32, :]
    gates, ahead, thinned, share, passing = segment_parts(raw_ref[...], gaps)
    for c in range(3):
        seg_ref[:, c : c + 1, :] = jnp.sum(share * gates[c], axis=1, keepdims=True)
    seg_ref[:, 3:4, :] = passing
    seg_ref[:, 4:, :] = jnp.zeros((held, 4, width), F32)
    terms = gates[:3] + [share * (gate * (1.0 - gate)) for gate in gates[:3]]
    terms += [share, ahead * thinned, gaps * gates[3]]
    for index, term in enumerate(terms):
        terms_ref[:, index * samples : (index + 1) * samples, :] = term
    for src in range(owners):
        lanes = slice(src * capacity, (src + 1) * capacity)
        send_ref[pl.ds(src, 4, stride=owners), :] = jnp.concatenate(
            [seg_ref[vol, 0:4, lanes] for vol in range(held)], axis=1
        )


def table_lane(place, slot_width, me, low, high):
    owner = place // slot_width
    apart = owner ^ me
    position = (apart % low) * high + apart // low
    return position * slot_width + (place - owner * slot_width)


def prepare_kernel(vols, order, slot_width, *refs):
    where_ref, slots_ref = refs[:2]
    stored = refs[2 : 2 + 4 * len(vols)]
    outs = refs[2 + 4 * len(vols) :]
    samples = 8
    width = slots_ref.shape[2]
    me = where_ref[1]
    hidden = stored[0].shape[1]
    eye = one_hot_rows(hidden, lax.broadcasted_iota(jnp.int32, (1, hidden), 1))
    for n, vol in enumerate(vols):
        slope_one_ref, slope_two_ref, hot_ref, act_t_ref = outs[4 * n : 4 * n + 4]
        act_one = stored[4 * n][0:width, :]
        turned = mm_nt(eye, act_one)
        for i in range(samples):
            rows = slice(i * width, (i + 1) * width)
            act_two, up_one, up_two = [ref[rows, :] for ref in stored[4 * n + 1 : 4 * n + 4]]
            if i + 1 < samples:
                act_next = stored[4 * n][(i + 1) * width : (i + 2) * width, :]
                turned_next = mm_nt(eye, act_next)
            slopes = []
            for act, up in ((act_one, up_one), (act_two, up_two)):
                slopes.append(up + act * (jnp.asarray(2.0, BF) - up))
            slope_one_ref[rows, :] = slopes[0]
            slope_two_ref[rows, :] = slopes[1]
            act_t_ref[:, rows] = turned.astype(BF)
            act_one, turned = act_next, turned_next
        partner = slots_ref[vol, 35:36, :].astype(jnp.int32)
        hot_ref[...] = one_hot_rows(hot_ref.shape[0], table_lane(partner, slot_width, me, *order))


def gathered(all_ref, owners):
    count = all_ref.shape[0] // owners
    return split3(
        jnp.concatenate([all_ref[n * count : (n + 1) * count] for n in range(owners)], axis=1)
    )


def look_up(pieces, hot, owners, is_source):
    found = join3(mm(pieces, hot), 4 * owners)
    return [
        jnp.sum(
            jnp.where(is_source, found[c * owners : (c + 1) * owners], 0.0), axis=0, keepdims=True
        )
        for c in range(4)
    ]


def color_kernel(owners, order, slot_width, where_ref, place_ref, all_ref, color_ref):
    rays = color_ref.shape[1]
    hot = one_hot_rows(
        owners * slot_width, table_lane(place_ref[...], slot_width, where_ref[1], *order)
    )
    own_row = lax.broadcasted_iota(jnp.int32, (owners, 2 * rays), 0) == where_ref[1]
    values = look_up(gathered(all_ref, owners), hot, owners, own_row)
    for c in range(3):
        color_ref[c : c + 1, :] = values[c][:, :rays] + values[3][:, :rays] * values[c][:, rays:]


def cotangents(
    capacity, owners, replicas, all_ref, slots_ref, seg_ref, terms_ref, hot_refs, cots_ref
):
    samples = 8
    width = owners * capacity
    pieces = gathered(all_ref, owners)
    source = lax.broadcasted_iota(jnp.int32, (owners, width), 1) // capacity
    is_source = lax.broadcasted_iota(jnp.int32, (owners, width), 0) == source

    for vol in range(slots_ref.shape[0]):
        extra = slots_ref[vol, 32:40, :]
        other = look_up(pieces, hot_refs[vol][...], owners, is_source)
        seg = seg_ref[vol]
        own = [seg[c : c + 1] for c in range(4)]
        is_second = extra[4:5] > 0.5
        cot_color = []
        cot_pass = jnp.zeros((1, width), F32)
        for c in range(3):
            color = jnp.where(
                is_second, other[c] + other[3] * own[c], own[c] + own[3] * other[c]
            )
            cot = (color - extra[c : c + 1]) / replicas
            cot_color.append(jnp.where(is_second, cot * other[3], cot))
            cot_pass = cot_pass + cot * other[c]
        cot_pass = jnp.where(is_second, 0.0, cot_pass)

        terms = [
            terms_ref[vol, index * samples : (index + 1) * samples, :] for index in range(9)
        ]
        pull = jnp.zeros((samples, width), F32)
        raw_cots = []
        for c in range(3):
            pull = pull + cot_color[c] * terms[c]
            raw_cots.append(cot_color[c] * terms[3 + c])
        weighted = pull * terms[6]
        behind = [jnp.zeros((1, width), F32)]
        for sample in range(samples - 1, 0, -1):
            behind.insert(0, behind[0] + weighted[sample : sample + 1])
        cot_tau = pull * terms[7] - jnp.concatenate(behind, axis=0) - cot_pass * own[3]
        raw_cots.append(cot_tau * terms[8])
        for i in range(samples):
            cots_ref[vol, :, i * width : (i + 1) * width] = jnp.concatenate(
                [raw_cots[c][i : i + 1] for c in range(4)] + [jnp.zeros((4, width), F32)], axis=0
            )


def backward_kernel(capacity, owners, replicas, vols, given, form, *refs):
    where_ref, w2_ref, w3_ref, enc_t_ref = refs[:4]
    prepared = [refs[4 + 4 * n : 8 + 4 * n] for n in range(len(vols))]
    rest = refs[4 + 4 * len(vols) :]
    if form == "pairs":
        held = w2_ref.shape[0]
        sources, rest = rest[: 4 + held], rest[4 + held :]
    else:
        cots_ref, rest = rest[0], rest[1:]
    given_refs, rest = rest[: 3 * given], rest[3 * given :]
    out_refs, grad_hidden_s = rest[:-1], rest[-1]
    if form == "pairs":
        cots_ref, out_refs = out_refs[-1], out_refs[:-1]
        cotangents(capacity, owners, replicas, *sources[:4], sources[4:], cots_ref)
    hidden = w2_ref.shape[1]
    features = enc_t_ref.shape[1]
    samples = 8
    width = owners * capacity
    block = hidden // replicas
    group = where_ref[0]

    def last(n, vol, i):
        cots = cots_ref[vol, :, i * width : (i + CHUNK) * width].T.astype(BF)
        return mm(cots, w3_ref[vol])

    order = [(n, vol, i) for n, vol in enumerate(vols) for i in range(0, samples, CHUNK)]
    pulled = last(*order[0])
    hiddens, ins, heads = [], [], []
    for at, (n, vol, i) in enumerate(order):
        rows = slice(i * width, (i + CHUNK) * width)
        act_two_ref, slope_one_ref, slope_two_ref, act_t_ref = prepared[n]
        slope_one, slope_two = slope_one_ref[rows, :], slope_two_ref[rows, :]
        act_two = act_two_ref[rows, :]
        act_t, enc_t, w2 = act_t_ref[:, rows], enc_t_ref[vol, :, rows], w2_ref[vol]
        cots = cots_ref[vol, :, rows].astype(BF)
        ahead = last(*order[at + 1]) if at + 1 < len(order) else None
        cot_two = pulled.astype(BF) * slope_two
        cot_one = mm_nt(cot_two, w2)
        sums = [mm(act_t, cot_two), mm(cots, act_two)]
        sums.append(mm(enc_t, cot_one.astype(BF) * slope_one))
        for total, part in zip((hiddens, heads, ins), sums):
            if i == 0:
                total.append(part)
            else:
                total[n] = total[n] + part
        pulled = ahead
    for n in range(len(vols)):
        grad_hidden_s[n] = hiddens[n]

    if form == "raw":
        for n in range(len(vols)):
            out_refs[3 * n][...] = grad_hidden_s[n]
            out_refs[3 * n + 1][...] = ins[n]
            out_refs[3 * n + 2][...] = heads[n]
        return
    hiddens = [given_refs[3 * n] for n in range(given)]
    hiddens += [grad_hidden_s.at[n] for n in range(len(vols))]
    ins = [given_refs[3 * n + 1][...] for n in range(given)] + ins
    heads = [given_refs[3 * n + 2][...] for n in range(given)] + heads
    count = len(hiddens)
    base = count * block
    half = features // 2
    if form == "pairs":
        targets = [
            (out_refs[way].at[k], group ^ way, 2 * k)
            for way in range(2)
            for k in range(replicas // 2)
        ]
    else:
        targets = [(out_refs[k], group, k) for k in range(replicas)]
    for out_ref, start, k in targets:
        to = pl.ds(pl.multiple_of(lax.rem(start + k, replicas) * block, block), block)
        for n in range(count):
            out_ref[n * block : (n + 1) * block, :] = hiddens[n][to, :].astype(BF)
        turn = jnp.where(start == 0, 0, hidden - start * block)
        cols = slice(k * block, (k + 1) * block)
        parts = [
            pltpu.roll(grad, turn, 1)[h * half : (h + 1) * half, cols]
            for grad in ins
            for h in range(2)
        ]
        out_ref[base : base + half, : 2 * count * block] = jnp.concatenate(parts, axis=1).astype(BF)
        head = jnp.concatenate([pltpu.roll(grad, turn, 1)[:, cols] for grad in heads], axis=1)
        out_ref[base + half :, : count * block] = jnp.concatenate(
            [head, jnp.zeros_like(head)], axis=0
        ).astype(BF)


def sum_kernel(addends, *refs):
    grad_in_ref, grad_hidden_ref, grad_head_ref = refs[-3:]
    held, features, block = grad_in_ref.shape
    half = features // 2
    count = held // len(addends)
    base = count * block
    start = 0
    for part, number in enumerate(addends):
        pieces = refs[start : start + number]
        start += number
        total = pieces[0][...].astype(F32)
        for piece in pieces[1:]:
            total = total + piece[...].astype(F32)
        for v in range(count):
            vol = part * count + v
            grad_hidden_ref[vol] = total[v * block : (v + 1) * block]
            for h in range(2):
                cols = slice((2 * v + h) * block, (2 * v + h + 1) * block)
                grad_in_ref[vol, h * half : (h + 1) * half, :] = total[base : base + half, cols]
            grad_head_ref[vol] = total[base + half : base + half + 4, v * block : (v + 1) * block]


VMEM = pl.BlockSpec(memory_space=pltpu.VMEM)
SMEM = pl.BlockSpec(memory_space=pltpu.SMEM)
HBM = pl.BlockSpec(memory_space=pltpu.HBM)


def call(kernel, specs, inputs, out_shape, scratch=(), limit=16, flops=0, out_space=VMEM):
    return pl.pallas_call(
        kernel,
        out_shape=out_shape,
        in_specs=list(specs),
        out_specs=jax.tree.map(lambda _: out_space, out_shape),
        scratch_shapes=list(scratch),
        compiler_params=pltpu.CompilerParams(vmem_limit_bytes=limit << 20),
        cost_estimate=pl.CostEstimate(flops=flops, bytes_accessed=flops >> 10, transcendentals=0),
    )(*inputs)


def steps(count, size):
    return [(at, (at + count) % size) for at in range(size)]


def local(positions, spacing, volume_ids, target, w_in, w_hidden, w_head):
    rays, seg_count = volume_ids.shape
    samples = spacing.shape[2]
    owners = lax.axis_size("vol")
    replicas = lax.axis_size("rep")
    held, features, hidden = w_in.shape
    volume_count = owners * held
    capacity = 2 * rays * seg_count // volume_count
    slot_width = held * capacity
    width = owners * capacity
    rows = width * samples
    shape = jax.ShapeDtypeStruct
    where = jnp.stack([lax.axis_index("rep"), lax.axis_index("vol")]).astype(jnp.int32)

    outgoing, place = call(
        functools.partial(dispatch_kernel, volume_count, capacity),
        [HBM] * 4,
        (
            jnp.transpose(positions, (1, 2, 0)),
            jnp.transpose(spacing, (1, 2, 0)),
            volume_ids.T,
            target,
        ),
        (
            shape((owners, PAYLOAD, slot_width), F32),
            shape((1, rays * seg_count), jnp.int32),
        ),
        limit=60,
        scratch=(
            pltpu.VMEM((seg_count, COORDS * samples, rays), F32),
            pltpu.VMEM((seg_count, samples, rays), F32),
            pltpu.VMEM((seg_count, rays), jnp.int32),
            pltpu.VMEM((3, rays), F32),
            pltpu.VMEM((owners, PAYLOAD, slot_width), F32),
            pltpu.VMEM((1, rays * seg_count), jnp.int32),
            pltpu.SemaphoreType.DMA((7,)),
        ),
        out_space=HBM,
    )
    outgoing, late_in, late_hidden, late_head, zero = lax.optimization_barrier(
        (outgoing, w_in, w_hidden, w_head, jnp.zeros((), jnp.int32))
    )
    arrived = lax.all_to_all(outgoing, "vol", split_axis=0, concat_axis=0, tiled=True)
    half = jnp.asarray(0.5, BF)
    half_in = late_in * half
    pair = jnp.pad(half_in, ((0, 0), (0, features), (0, hidden))) + jnp.pad(
        half_in, ((0, 0), (features, 0), (hidden, 0))
    )
    half_hidden, half_head = late_hidden * half, late_head * half
    w_head_t = lax.pad(
        jnp.swapaxes(half_head, 1, 2),
        jnp.zeros((), BF),
        ((0, 0, 0), (0, 0, 0), (0, 127 - 3 * samples, samples - 1)),
    )
    w_head_8 = jnp.pad(half_head, ((0, 0), (0, 4), (0, 0)))
    slots, enc_t, seg, gathering, terms, *stored = call(
        functools.partial(forward_kernel, capacity),
        [VMEM] * 5,
        (arrived, selection(samples, zero), pair, half_hidden, w_head_t),
        (
            shape((held, PAYLOAD, width), F32),
            shape((held, features, rows), BF),
            shape((held, 8, width), F32),
            shape((4 * owners, slot_width), F32),
            shape((held, 9 * samples, width), F32),
        )
        + (shape((rows, hidden), BF),) * (4 * held),
        scratch=(pltpu.VMEM((held, 4 * samples, width), F32),),
        flops=10**10,
    )

    low = 1 << ((owners.bit_length() - 1) // 2)
    high = owners // low
    order = (low, high)
    prepared, hots = {}, {}
    for stage, (stride, count) in enumerate(((low, high), (1, low))):
        received = [
            lax.ppermute(gathering, "vol", [(at, at ^ (n * stride)) for at in range(owners)])
            for n in range(count - 1, 0, -1)
        ][::-1]
        vols = list(range(stage * held // 2, (stage + 1) * held // 2))
        late_slots = lax.optimization_barrier((slots, gathering))[0] if stage else slots
        outs = call(
            functools.partial(prepare_kernel, vols, order, slot_width),
            [SMEM] + [VMEM] * (1 + 4 * len(vols)),
            (where, late_slots) + tuple(stored[4 * vols[0] : 4 * vols[-1] + 4]),
            (
                shape((rows, hidden), BF),
                shape((rows, hidden), BF),
                shape((volume_count * capacity, width), BF),
                shape((hidden, rows), BF),
            )
            * len(vols),
            flops=len(vols) * 3 * 10**9,
        )
        outs = tuple(outs)
        *received, first_out = lax.optimization_barrier(tuple(received) + (outs[2],))
        outs = outs[:2] + (first_out,) + outs[3:]
        for n, vol in enumerate(vols):
            slope_one, slope_two, hots[vol], act_t = outs[4 * n : 4 * n + 4]
            prepared[vol] = (stored[4 * vol + 1], slope_one, slope_two, act_t)
        gathering = jnp.concatenate([gathering] + received, axis=0)

    block = hidden // replicas
    count = held // 2
    send_rows = count * block + features // 2 + 16

    def backward(vols, given, form, outs):
        given = tuple(given)
        return call(
            functools.partial(
                backward_kernel, capacity, owners, replicas, vols, len(given) // 3, form
            ),
            [SMEM] + [VMEM] * (3 + 4 * len(vols) + len(sources) + len(given)),
            (where, half_hidden, w_head_8, enc_t)
            + sum((prepared[vol] for vol in vols), ())
            + sources
            + given,
            outs,
            scratch=(pltpu.VMEM((len(vols), hidden, hidden), F32),),
            flops=len(vols) * 5 * 10**9,
        )

    sources = (gathering, slots, seg, terms) + tuple(hots[vol] for vol in range(held))
    keep, give, cots = backward(
        list(range(count)),
        (),
        "pairs",
        (shape((replicas // 2, send_rows, hidden), BF),) * 2 + (shape((held, 8, rows), F32),),
    )
    sources = (cots,)
    received = lax.ppermute(give, "rep", [(at, at ^ 1) for at in range(replicas)])
    middle = list(range(count, held - 1))
    raw_grads = ()
    if middle:
        raw_grads = backward(
            middle,
            (),
            "raw",
            (
                shape((hidden, hidden), F32),
                shape((features, hidden), F32),
                shape((8, hidden), F32),
            )
            * len(middle),
        )
        received, *raw_grads = lax.optimization_barrier((received,) + tuple(raw_grads))
    total = keep.astype(F32) + received.astype(F32)
    pieces = [total[0]]
    for k in range(1, replicas // 2):
        pieces.append(lax.ppermute(total[k].astype(BF), "rep", steps(2 * k, replicas)))
    cots, raw_grads, total = lax.optimization_barrier((cots, raw_grads, total))
    sources = (cots,)
    outs = backward(
        [held - 1], raw_grads, "direct", (shape((send_rows, hidden), BF),) * replicas
    )
    pieces.append(outs[0])
    for k in range(1, replicas):
        pieces.append(lax.ppermute(outs[k], "rep", steps(k, replicas)))
    late, _ = lax.optimization_barrier((gathering, outs[0]))
    color = call(
        functools.partial(color_kernel, owners, order, slot_width),
        [SMEM, VMEM, VMEM],
        (where, place, late),
        shape((3, rays), F32),
    )
    grad_in, grad_hidden, grad_head = call(
        functools.partial(sum_kernel, (replicas // 2, replicas)),
        [VMEM] * len(pieces),
        pieces,
        (
            shape((held, features, block), F32),
            shape((held, block, hidden), F32),
            shape((held, 4, block), F32),
        ),
    )
    return color, grad_in, grad_hidden, grad_head


def solution(mesh):
    return jax.shard_map(
        local,
        mesh=mesh,
        in_specs=(
            P(("rep", "vol"), None, None),
            P(("rep", "vol"), None, None),
            P(("rep", "vol"), None),
            P(None, ("rep", "vol")),
            P("vol", None, None),
            P("vol", None, None),
            P("vol", None, None),
        ),
        out_specs=(
            P(None, ("rep", "vol")),
            P("vol", None, "rep"),
            P("vol", "rep", None),
            P("vol", None, "rep"),
        ),
        check_vma=False,
    )
```

time: 239 us -> 51.1 us (0.21)
  waiting for transfers between devices: 98.7 us -> 7.44 us
  matrix products: 45.2 us -> 0 us
  local copies, waits for them, and re-layouts: 30.5 us -> 2.16 us
  other arithmetic: 27.9 us -> 0.45 us
  Pallas kernels: 0 us -> 21.3 us
  between operations: 14.2 us -> 0.89 us
    dot_general x36 -> x0, matrix products: 45.2 us -> none  [product(): return jnp.dot(left, right, preferred_element_type=jnp.float32)]
    unnamed x5 -> x0, waiting for transfers between devices: 39.1 us -> none
    reduce_scatter x1 -> x0, waiting for transfers between devices: 26.4 us -> none  [local(): lax.psum_scatter(partial_grads[1], 'rep', scatter_dimension=1, tiled=True)]
    pallas_call x0 -> x9, Pallas kernels: none -> 21.3 us  [call(): pl.pallas_call(kernel, out_shape=out_shape, in_specs=list(specs), out_spe...]
    all_to_all x1, waiting for transfers between devices: 23.3 us -> 4.49 us  [local(): lax.all_to_all(outgoing, 'vol', split_axis=0, concat_axis=0, tiled=True)]
    all_to_all x3 -> x0, starting transfers between devices: 14.8 us -> none  [the longest x1 6.35 us: local(): lax.all_to_all(gap_slots.astype(jnp.bfloat16), 'vol', split_axis=0, conca...]
    another operation x6 -> x1, other arithmetic: 13.6 us -> 0.08 us  [local(): jnp.stack([lax.axis_index('rep'), lax.axis_index('vol')]).astype(jnp.int32)]
    ppermute x0 -> x9, starting transfers between devices: none -> 12 us  [the longest x4 5.12 us: local(): lax.ppermute(gathering, 'vol', [(at, at ^ n * stride) for at in range(own...]
  transfers between devices with their start and end apart: 7 -> 10, of which waited for: 6 -> 4; matrix products, arithmetic and copies ran while one was open for 6% -> 2% of each run, Pallas kernels for 0% -> 19%
where the time goes in v1:
time: 51.1 us; the launch traced here: 50.7 us
  Pallas kernels  21.3 us (42%)
  starting transfers between devices  18.5 us (36%)
  waiting for transfers between devices  7.44 us (15%)
  local copies, waits for them, and re-layouts  2.16 us (4%)
  between operations  0.89 us (2%)
    pallas_call x9, Pallas kernels, call(): pl.pallas_call(kernel, out_shape=out_shape, in_specs=list(specs), out_spe...  21.3 us
    all_to_all x1, starting transfers between devices, local(): lax.all_to_all(outgoing, 'vol', split_axis=0, concat_axis=0, tiled=True)  6.5 us
    ppermute x4, starting transfers between devices, local(): lax.ppermute(gathering, 'vol', [(at, at ^ n * stride) for at in range(own...  5.12 us
    all_to_all x1, waiting for transfers between devices, local(): lax.all_to_all(outgoing, 'vol', split_axis=0, concat_axis=0, tiled=True)  4.49 us
    ppermute x1, starting transfers between devices, local(): lax.ppermute(give, 'rep', [(at, at ^ 1) for at in range(replicas)])  3.87 us
    ppermute x3, waiting for transfers between devices, local(): pieces.append(lax.ppermute(outs[k], 'rep', steps(k, replicas)))  2.63 us
    ppermute x3, starting transfers between devices, local(): pieces.append(lax.ppermute(outs[k], 'rep', steps(k, replicas)))  1.7 us
    unnamed x12, local copies, waits for them, and re-layouts  1.55 us
  transfers between devices with their start and end apart: 10, of which 4 were waited for; matrix products, arithmetic and copies ran while one was open for 2% of the time, Pallas kernels for 19%

profile of v1, /device:TPU:1, one launch (start us, length us, event | category | flops | bytes accessed | tf_op | source)
XLA Modules:
  0.0 50.7 jit_solution(7305974504065272182)
XLA Ops:
  0.6 2.1 %shard_map.102 = (f32[8,40,128]{2,1,0:T(8,128)}, s32[1,512]{1,0:T(1,128)}) custom-call(f32[2,24,256]{2,1,0:T(8,128)} %bitcast.11, f32[2,8,256]{2,1,0:T(8,128)} %bitcast.12, s32[2,256]{1,0:T(2,128)} %bitcast.13, f32[3,256]{1,0:T(4,128)} %tgt_hbm.1), custom_call_target="tpu_custom_call" | custom-call | tf_op jit(solution)/shard_map/pallas_call | solution.py:522
  2.7 6.5 %all-to-all-start = ((f32[8,40,128]{2,1,0:T(8,128)}), f32[8,40,128]{2,1,0:T(8,128)S(1)}, u32[]{:S(2)}, u32[]{:S(2)}) async-start(f32[8,40,128]{2,1,0:T(8,128)} %get-tuple-element.79), calls=%async_computation | async-start | bytes 327680 | tf_op jit(solution)/shard_map/all_to_all | solution.py:579
  9.4 0.6 %copy-done.3 = bf16[4,4,256]{2,1,0:T(4,128)(2,1)S(1)} copy-done((bf16[4,4,256]{2,1,0:T(4,128)(2,1)S(1)}, bf16[4,4,256]{2,1,0:T(4,128)(2,1)}, u32[]{:S(2)}) %copy-start.3) | copy-done | bytes 8216
  10.5 0.6 %pad.17.clone.w3_ref = bf16[4,256,128]{2,1,0:T(8,128)(2,1)S(1)} pad(bf16[4,256,4]{2,1,0:T(8,128)(2,1)S(1)} %copy.12, bf16[]{:T(256)} %constant.89.clone.1), padding=0_0_0x0_0_0x0_103_7 | pad | bytes 270338 | tf_op jit(solution)/shard_map/pad | solution.py:586
  11.2 4.5 %all-to-all-done.in_ref = f32[8,40,128]{2,1,0:T(8,128)S(1)} async-done(((f32[8,40,128]{2,1,0:T(8,128)}), f32[8,40,128]{2,1,0:T(8,128)S(1)}, u32[]{:S(2)}, u32[]{:S(2)}) %all-to-all-start) | async-done | bytes 163872 | tf_op jit(solution)/shard_map/all_to_all | solution.py:579
  15.7 5.2 %shard_map.103 = (f32[4,40,256]{2,1,0:T(8,128)S(1)}, bf16[4,64,2048]{2,1,0:T(8,128)(2,1)S(1)}, f32[4,8,256]{2,1,0:T(8,128)S(1)}, f32[32,128]{1,0:T(8,128)S(1)}, ...) custom-call(f32[8,40,128]{2,1,0:T(8,128)S(1)} %all-to-all-done.in_re, ...), custom_call_target="tpu_custom_call" | custom-call | flops 10000000000 | bytes 9765625 | tf_op jit(solution)/shard_map/pallas_call | solution.py:522
  20.9 1.5 %collective-permute-start.1 = (f32[32,128]{1,0:T(8,128)S(1)}, f32[32,128]{1,0:T(8,128)S(1)}, u32[]{:S(2)}, u32[]{:S(2)}) collective-permute-start(f32[32,128]{1,0:T(8,128)S(1)} %get-tuple-element.84), channel_id=1, source_target_pairs={{0,4},{1,5},{2,6},{3,7},{4,0},{5,1},{6,2},{7,3},{8,12},{9,13},{10,... | collective-permute-start | bytes 49160 | tf_op jit(solution)/shard_map/ppermute | solution.py:614
  22.4 2.0 %collective-permute-start.2 = (f32[32,128]{1,0:T(8,128)S(1)}, f32[32,128]{1,0:T(8,128)S(1)}, u32[]{:S(2)}, u32[]{:S(2)}) collective-permute-start(f32[32,128]{1,0:T(8,128)S(1)} %get-tuple-element.84), channel_id=1, source_target_pairs={{0,6},{1,7},{2,4},{3,5},{4,2},{5,3},{6,0},{7,1},{8,14},{9,15},{10,... | collective-permute-start | bytes 49160 | tf_op jit(solution)/shard_map/ppermute | solution.py:614
  24.4 2.0 %shard_map.104 = (bf16[2048,256]{1,0:T(8,128)(2,1)S(1)}, bf16[2048,256]{1,0:T(8,128)(2,1)S(1)}, bf16[1024,256]{1,0:T(8,128)(2,1)S(1)}, bf16[256,2048]{1,0:T(8,12...) custom-call(s32[2]{0:T(128)S(1)} %pad_add_fusion.1.refs_0_.where_ref, ...), custom_call_target="tpu_custom_call" | custom-call | flops 6000000000 | bytes 5859375 | tf_op jit(solution)/shard_map/pallas_call | solution.py:522
  26.5 0.3 collective-permute-done.2
  26.8 1.6 %collective-permute-start.3 = (f32[128,128]{1,0:T(8,128)S(1)}, f32[128,128]{1,0:T(8,128)S(1)}, u32[]{:S(2)}, u32[]{:S(2)}) collective-permute-start(f32[128,128]{1,0:T(8,128)S(1)} %get-tuple-element.150), channel_id=1, source_target_pairs={{0,1},{1,0},{2,3},{3,2},{4,5},{5,4},{6,7},{7,6},{8,9},{9,8},{10,11... | collective-permute-start | bytes 196616 | tf_op jit(solution)/shard_map/ppermute | solution.py:614
  28.4 2.0 %shard_map.105 = (bf16[2048,256]{1,0:T(8,128)(2,1)S(1)}, bf16[2048,256]{1,0:T(8,128)(2,1)S(1)}, bf16[1024,256]{1,0:T(8,128)(2,1)S(1)}, bf16[256,2048]{1,0:T(8,12...) custom-call(s32[2]{0:T(128)S(1)} %pad_add_fusion.1.refs_0_.where_ref, ...), custom_call_target="tpu_custom_call" | custom-call | flops 6000000000 | bytes 5859375 | tf_op jit(solution)/shard_map/pallas_call | solution.py:522
  30.5 3.7 %shard_map.106 = (bf16[2,176,256]{2,1,0:T(8,128)(2,1)S(1)}, bf16[2,176,256]{2,1,0:T(8,128)(2,1)S(1)}, f32[4,8,2048]{2,1,0:T(8,128)S(1)}) custom-call(s32[2]{0:T(128)S(1)} %pad_add_fusion.1.refs_0_.where_ref, bf16[4,256,256]{2,1,0:T(8,128)(2,1)S(1)} %broadcast_multiply_fusion.w2_ref.refs_1_, bf16[4,8,256]{2,1,0:T(8,128)(2,1)S(1)} %pad.18.refs_2_, ...), custom_call_target="tpu_custom_call" | custom-call | flops 10000000000 | bytes 9765625 | tf_op jit(solution)/shard_map/pallas_call | solution.py:522
  34.2 3.9 %collective-permute-start.4 = (bf16[2,176,256]{2,1,0:T(8,128)(2,1)S(1)}, bf16[2,176,256]{2,1,0:T(8,128)(2,1)S(1)}, u32[]{:S(2)}, u32[]{:S(2)}) collective-permute-start(bf16[2,176,256]{2,1,0:T(8,128)(2,1)S(1)} %get-tuple-element.126), channel_id=1, source_target_pairs={{0,8},{8,0},{16,24},{24,16},{1,9},{9,1},{17,25},{25,17},{2,10},{10... | collective-permute-start | bytes 540680 | tf_op jit(solution)/shard_map/ppermute | solution.py:668
  38.1 1.9 %shard_map.107 = (f32[256,256]{1,0:T(8,128)S(1)}, f32[64,256]{1,0:T(8,128)S(1)}, f32[8,256]{1,0:T(8,128)S(1)}) custom-call(s32[2]{0:T(128)S(1)} %pad_add_fusion.1.refs_0_.where_ref, bf16[4,256,256]{2,1,0:T(8,128)(2,1)S(1)} %broadcast_multiply_fusion.w2_ref.refs_1_, bf16[4,8,256]{2,1,0:T(8,128)(2,1)S(1)} %pad.18.refs_2_, ...), custom_call_target="tpu_custom_call" | custom-call | flops 5000000000 | bytes 4882812 | tf_op jit(solution)/shard_map/pallas_call | solution.py:522
  40.0 1.3 %collective-permute-start.5 = (bf16[176,256]{1,0:T(8,128)(2,1)S(1)}, bf16[176,256]{1,0:T(8,128)(2,1)S(1)}, u32[]{:S(2)}, u32[]{:S(2)}) collective-permute-start(bf16[176,256]{1,0:T(8,128)(2,1)S(1)} %fusion.22), channel_id=1, source_target_pairs={{0,16},{8,24},{16,0},{24,8},{1,17},{9,25},{17,1},{25,9},{2,18},{10... | collective-permute-start | bytes 270344 | tf_op jit(solution)/shard_map/ppermute | solution.py:687
  41.3 2.1 %shard_map.108 = (bf16[176,256]{1,0:T(8,128)(2,1)S(1)}, bf16[176,256]{1,0:T(8,128)(2,1)S(1)}, bf16[176,256]{1,0:T(8,128)(2,1)S(1)}, bf16[176,256]{1,0:T(8,128)(2,1)S(1)}) custom-call(s32[2]{0:T(128)S(1)} %pad_add_fusion.1.refs_0_.where_ref, bf16[4,256,256]{2,1,0:T(8,128)(2,1)S(1)} %broadcast_multiply_fusion.w2_ref.refs_1_, ...), custom_call_target="tpu_custom_call" | custom-call | flops 5000000000 | bytes 4882812 | tf_op jit(solution)/shard_map/pallas_call | solution.py:522
  43.4 0.5 collective-permute-start.6
  43.9 1.2 %collective-permute-start.7 = (bf16[176,256]{1,0:T(8,128)(2,1)S(1)}, bf16[176,256]{1,0:T(8,128)(2,1)S(1)}, u32[]{:S(2)}, u32[]{:S(2)}) collective-permute-start(bf16[176,256]{1,0:T(8,128)(2,1)S(1)} %get-tuple-element.145), channel_id=1, source_target_pairs={{0,16},{8,24},{16,0},{24,8},{1,17},{9,25},{17,1},{25,9},{2,18},{10... | collective-permute-start | bytes 270344 | tf_op jit(solution)/shard_map/ppermute | solution.py:695
  45.1 0.7 %copy-done = s32[1,512]{1,0:T(1,128)S(1)} copy-done((s32[1,512]{1,0:T(1,128)S(1)}, s32[1,512]{1,0:T(1,128)}, u32[]{:S(2)}) %copy-start) | copy-done | bytes 2072
  45.8 1.5 %shard_map.109 = f32[3,256]{1,0:T(4,128)} custom-call(s32[2]{0:T(128)S(1)} %pad_add_fusion.1.refs_0_.where_ref, s32[1,512]{1,0:T(1,128)S(1)} %copy-done, f32[256,128]{1,0:T(8,128)S(1)} %constant_dynamic-update-slice_fusion.4.refs_12_.all_ref), custom_call_target="tpu_custom_call" | custom-call | tf_op jit(solution)/shard_map/pallas_call | solution.py:522
  47.3 1.9 %collective-permute-done.7.refs_4_ = bf16[176,256]{1,0:T(8,128)(2,1)S(1)} collective-permute-done((bf16[176,256]{1,0:T(8,128)(2,1)S(1)}, bf16[176,256]{1,0:T(8,128)(2,1)S(1)}, u32[]{:S(2)}, u32[]{:S(2)}) %collective-permute-start.7) | collective-permute-done | bytes 90144 | tf_op jit(solution)/shard_map/ppermute | solution.py:695
  49.2 0.8 %collective-permute-done.8.refs_5_ = bf16[176,256]{1,0:T(8,128)(2,1)S(1)} collective-permute-done((bf16[176,256]{1,0:T(8,128)(2,1)S(1)}, bf16[176,256]{1,0:T(8,128)(2,1)S(1)}, u32[]{:S(2)}, u32[]{:S(2)}) %collective-permute-start.8) | collective-permute-done | bytes 90144 | tf_op jit(solution)/shard_map/ppermute | solution.py:695
  49.9 0.8 %shard_map.110 = (f32[4,64,64]{2,1,0:T(8,128)}, f32[4,64,256]{2,1,0:T(8,128)}, f32[4,4,64]{2,1,0:T(4,128)}) custom-call(f32[176,256]{1,0:T(8,128)S(1)} %slice_bitcast_fusion.refs_0_, bf16[176,256]{1,0:T(8,128)(2,1)S(1)} %collective-permute-done.5.refs_1_, bf16[176,256]{1,0:T(8,128)(2,1)S(1)} %get-tuple-element.142.refs_2_, ...), custom_call_target="tpu_custom_call" | custom-call | tf_op jit(solution)/shard_map/pallas_call | solution.py:522
  (36 shorter events, 0.8 us)
Async XLA Ops:
  2.7 6.6 %copy-start.2 = (bf16[4,64,256]{2,1,0:T(8,128)(2,1)S(1)}, bf16[4,64,256]{2,1,0:T(8,128)(2,1)}, u32[]{:S(2)}) copy-start(bf16[4,64,256]{2,1,0:T(8,128)(2,1)} %param.11) | copy-start | bytes 393220
  2.7 12.9 %all-to-all-start = ((f32[8,40,128]{2,1,0:T(8,128)}), f32[8,40,128]{2,1,0:T(8,128)S(1)}, u32[]{:S(2)}, u32[]{:S(2)}) async-start(f32[8,40,128]{2,1,0:T(8,128)} %get-tuple-element.79), calls=%async_computation | async-start | bytes 327680 | tf_op jit(solution)/shard_map/all_to_all | solution.py:579
  9.3 0.7 %copy-start.3 = (bf16[4,4,256]{2,1,0:T(4,128)(2,1)S(1)}, bf16[4,4,256]{2,1,0:T(4,128)(2,1)}, u32[]{:S(2)}) copy-start(bf16[4,4,256]{2,1,0:T(4,128)(2,1)} %param.13) | copy-start | bytes 24580
  10.0 1.1 %copy-start.1 = (bf16[4,256,256]{2,1,0:T(8,128)(2,1)S(1)}, bf16[4,256,256]{2,1,0:T(8,128)(2,1)}, u32[]{:S(2)}) copy-start(bf16[4,256,256]{2,1,0:T(8,128)(2,1)} %param.12) | copy-start | bytes 1572868
  20.9 5.6 %collective-permute-start = (f32[32,128]{1,0:T(8,128)S(1)}, f32[32,128]{1,0:T(8,128)S(1)}, u32[]{:S(2)}, u32[]{:S(2)}) collective-permute-start(f32[32,128]{1,0:T(8,128)S(1)} %get-tuple-element.84), channel_id=1, source_target_pairs={{0,2},{1,3},{2,0},{3,1},{4,6},{5,7},{6,4},{7,5},{8,10},{9,11},{10,... | collective-permute-start | bytes 49160 | tf_op jit(solution)/shard_map/ppermute | solution.py:614
  20.9 5.6 %collective-permute-start.1 = (f32[32,128]{1,0:T(8,128)S(1)}, f32[32,128]{1,0:T(8,128)S(1)}, u32[]{:S(2)}, u32[]{:S(2)}) collective-permute-start(f32[32,128]{1,0:T(8,128)S(1)} %get-tuple-element.84), channel_id=1, source_target_pairs={{0,4},{1,5},{2,6},{3,7},{4,0},{5,1},{6,2},{7,3},{8,12},{9,13},{10,... | collective-permute-start | bytes 49160 | tf_op jit(solution)/shard_map/ppermute | solution.py:614
  22.4 4.4 %collective-permute-start.2 = (f32[32,128]{1,0:T(8,128)S(1)}, f32[32,128]{1,0:T(8,128)S(1)}, u32[]{:S(2)}, u32[]{:S(2)}) collective-permute-start(f32[32,128]{1,0:T(8,128)S(1)} %get-tuple-element.84), channel_id=1, source_target_pairs={{0,6},{1,7},{2,4},{3,5},{4,2},{5,3},{6,0},{7,1},{8,14},{9,15},{10,... | collective-permute-start | bytes 49160 | tf_op jit(solution)/shard_map/ppermute | solution.py:614
  26.8 3.6 %collective-permute-start.3 = (f32[128,128]{1,0:T(8,128)S(1)}, f32[128,128]{1,0:T(8,128)S(1)}, u32[]{:S(2)}, u32[]{:S(2)}) collective-permute-start(f32[128,128]{1,0:T(8,128)S(1)} %get-tuple-element.150), channel_id=1, source_target_pairs={{0,1},{1,0},{2,3},{3,2},{4,5},{5,4},{6,7},{7,6},{8,9},{9,8},{10,11... | collective-permute-start | bytes 196616 | tf_op jit(solution)/shard_map/ppermute | solution.py:614
  34.2 5.8 %collective-permute-start.4 = (bf16[2,176,256]{2,1,0:T(8,128)(2,1)S(1)}, bf16[2,176,256]{2,1,0:T(8,128)(2,1)S(1)}, u32[]{:S(2)}, u32[]{:S(2)}) collective-permute-start(bf16[2,176,256]{2,1,0:T(8,128)(2,1)S(1)} %get-tuple-element.126), channel_id=1, source_target_pairs={{0,8},{8,0},{16,24},{24,16},{1,9},{9,1},{17,25},{25,17},{2,10},{10... | collective-permute-start | bytes 540680 | tf_op jit(solution)/shard_map/ppermute | solution.py:668
  40.0 7.3 %collective-permute-start.5 = (bf16[176,256]{1,0:T(8,128)(2,1)S(1)}, bf16[176,256]{1,0:T(8,128)(2,1)S(1)}, u32[]{:S(2)}, u32[]{:S(2)}) collective-permute-start(bf16[176,256]{1,0:T(8,128)(2,1)S(1)} %fusion.22), channel_id=1, source_target_pairs={{0,16},{8,24},{16,0},{24,8},{1,17},{9,25},{17,1},{25,9},{2,18},{10... | collective-permute-start | bytes 270344 | tf_op jit(solution)/shard_map/ppermute | solution.py:687
  43.4 3.9 %collective-permute-start.6 = (bf16[176,256]{1,0:T(8,128)(2,1)S(1)}, bf16[176,256]{1,0:T(8,128)(2,1)S(1)}, u32[]{:S(2)}, u32[]{:S(2)}) collective-permute-start(bf16[176,256]{1,0:T(8,128)(2,1)S(1)} %get-tuple-element.144), channel_id=1, source_target_pairs={{0,8},{8,16},{16,24},{24,0},{1,9},{9,17},{17,25},{25,1},{2,10},{10... | collective-permute-start | bytes 270344 | tf_op jit(solution)/shard_map/ppermute | solution.py:695
  43.9 5.3 %collective-permute-start.7 = (bf16[176,256]{1,0:T(8,128)(2,1)S(1)}, bf16[176,256]{1,0:T(8,128)(2,1)S(1)}, u32[]{:S(2)}, u32[]{:S(2)}) collective-permute-start(bf16[176,256]{1,0:T(8,128)(2,1)S(1)} %get-tuple-element.145), channel_id=1, source_target_pairs={{0,16},{8,24},{16,0},{24,8},{1,17},{9,25},{17,1},{25,9},{2,18},{10... | collective-permute-start | bytes 270344 | tf_op jit(solution)/shard_map/ppermute | solution.py:695
  45.1 4.8 %collective-permute-start.8 = (bf16[176,256]{1,0:T(8,128)(2,1)S(1)}, bf16[176,256]{1,0:T(8,128)(2,1)S(1)}, u32[]{:S(2)}, u32[]{:S(2)}) collective-permute-start(bf16[176,256]{1,0:T(8,128)(2,1)S(1)} %get-tuple-element.146), channel_id=1, source_target_pairs={{0,24},{8,0},{16,8},{24,16},{1,25},{9,1},{17,9},{25,17},{2,26},{10... | collective-permute-start | bytes 270344 | tf_op jit(solution)/shard_map/ppermute | solution.py:695
  45.1 0.7 %copy-start = (s32[1,512]{1,0:T(1,128)S(1)}, s32[1,512]{1,0:T(1,128)}, u32[]{:S(2)}) copy-start(s32[1,512]{1,0:T(1,128)} %get-tuple-element.77.place_ref) | copy-start | bytes 6148

commit v2 on v1

--- a/solution.py
+++ b/solution.py
@@ -195,7 +195,7 @@
     w2_ref,
     w3_ref,
     slots_ref,
-    enc_t_ref,
+    enc_ref,
     seg_ref,
     send_ref,
     terms_ref,
@@ -207,14 +207,14 @@
     features = pair_ref.shape[1] // 2
     samples = 8
     width = owners * capacity
-    for vol in range(held):
+    lane = lax.broadcasted_iota(jnp.int32, (1, 128), 1)
+    plain = lax.broadcasted_iota(jnp.int32, (1, samples * features), 1) % features >= 60
+
+    def encode(vol):
         for src in range(owners):
             slots_ref[vol, :, src * capacity : (src + 1) * capacity] = in_ref[
                 src, :, vol * capacity : (vol + 1) * capacity
             ]
-    plain = lax.broadcasted_iota(jnp.int32, (1, samples * features), 1) % features >= 60
-
-    def encode(vol):
         pieces = split3(slots_ref[vol, 0:24, :]).astype(F32)
         points = jnp.concatenate(
             [pieces, jnp.ones((8, width), F32), jnp.zeros((48, width), F32)], axis=0
@@ -243,12 +243,8 @@
             half_one[step] = first(enc[vol], i, pair_ref[vol])
             if i == 0 and vol + 1 < held:
                 enc[vol + 1] = encode(vol + 1)
-            turned = enc[vol][:, i * features : (i + FORWARD_CHUNK) * features].T
-            for j in range(FORWARD_CHUNK):
-                lanes = pl.ds((i + j) * width, width)
-                stores.append(
-                    (enc_t_ref.at[vol, :, lanes], turned[j * features : (j + 1) * features])
-                )
+            if i == 0:
+                stores.append((enc_ref.at[vol], enc[vol]))
         at = step - 2
         if 0 <= at < len(order):
             half_two[at] = mm(act_one.pop(at), w2_ref[order[at][0]])
@@ -266,10 +262,16 @@
             rows = pl.ds(i * width, FORWARD_CHUNK * width)
             stores.append((stored[4 * vol + 1].at[rows, :], act_two))
             stores.append((stored[4 * vol + 3].at[rows, :], up))
-            values = mm(act_two, w3_ref[vol])
-            for j in range(FORWARD_CHUNK):
-                part = values[j * width : (j + 1) * width]
-                raw = part if i + j == 0 else raw + pltpu.roll(part, i + j, 1)
+            side = jnp.concatenate(
+                [act_two[j * width : (j + 1) * width] for j in range(FORWARD_CHUNK)], axis=1
+            )
+            spread = w3_ref[vol]
+            layers = [
+                jnp.where(lane % samples == i + j, spread, jnp.zeros((), BF))
+                for j in range(FORWARD_CHUNK)
+            ]
+            part = mm(side, jnp.concatenate(layers, axis=0))
+            raw = part if i == 0 else raw + part
             if i + FORWARD_CHUNK == samples:
                 stores.append((raw_ref.at[vol], raw.T[: 4 * samples]))
         for ref, value in stores:
@@ -300,16 +302,17 @@
 
 
 def prepare_kernel(vols, order, slot_width, *refs):
-    where_ref, slots_ref = refs[:2]
-    stored = refs[2 : 2 + 4 * len(vols)]
-    outs = refs[2 + 4 * len(vols) :]
+    where_ref, slots_ref, enc_ref = refs[:3]
+    stored = refs[3 : 3 + 4 * len(vols)]
+    outs = refs[3 + 4 * len(vols) :]
     samples = 8
     width = slots_ref.shape[2]
     me = where_ref[1]
     hidden = stored[0].shape[1]
     eye = one_hot_rows(hidden, lax.broadcasted_iota(jnp.int32, (1, hidden), 1))
     for n, vol in enumerate(vols):
-        slope_one_ref, slope_two_ref, hot_ref, act_t_ref = outs[4 * n : 4 * n + 4]
+        slope_one_ref, slope_two_ref, hot_ref, act_t_ref, enc_t_ref = outs[5 * n : 5 * n + 5]
+        features = enc_t_ref.shape[0]
         act_one = stored[4 * n][0:width, :]
         turned = mm_nt(eye, act_one)
         for i in range(samples):
@@ -324,6 +327,11 @@
             slope_one_ref[rows, :] = slopes[0]
             slope_two_ref[rows, :] = slopes[1]
             act_t_ref[:, rows] = turned.astype(BF)
+            if i % 2 == 0:
+                enc = enc_ref[vol, :, i * features : (i + 2) * features].T
+                for j in range(2):
+                    lanes = slice((i + j) * width, (i + j + 1) * width)
+                    enc_t_ref[:, lanes] = enc[j * features : (j + 1) * features]
             act_one, turned = act_next, turned_next
         partner = slots_ref[vol, 35:36, :].astype(jnp.int32)
         hot_ref[...] = one_hot_rows(hot_ref.shape[0], table_lane(partner, slot_width, me, *order))
@@ -366,7 +374,7 @@
     source = lax.broadcasted_iota(jnp.int32, (owners, width), 1) // capacity
     is_source = lax.broadcasted_iota(jnp.int32, (owners, width), 0) == source
 
-    for vol in range(slots_ref.shape[0]):
+    def volume(vol):
         extra = slots_ref[vol, 32:40, :]
         other = look_up(pieces, hot_refs[vol][...], owners, is_source)
         seg = seg_ref[vol]
@@ -402,11 +410,13 @@
                 [raw_cots[c][i : i + 1] for c in range(4)] + [jnp.zeros((4, width), F32)], axis=0
             )
 
+    return volume
+
 
 def backward_kernel(capacity, owners, replicas, vols, given, form, *refs):
-    where_ref, w2_ref, w3_ref, enc_t_ref = refs[:4]
-    prepared = [refs[4 + 4 * n : 8 + 4 * n] for n in range(len(vols))]
-    rest = refs[4 + 4 * len(vols) :]
+    where_ref, w2_ref, w3_ref = refs[:3]
+    prepared = [refs[3 + 5 * n : 8 + 5 * n] for n in range(len(vols))]
+    rest = refs[3 + 5 * len(vols) :]
     if form == "pairs":
         held = w2_ref.shape[0]
         sources, rest = rest[: 4 + held], rest[4 + held :]
@@ -416,9 +426,13 @@
     out_refs, grad_hidden_s = rest[:-1], rest[-1]
     if form == "pairs":
         cots_ref, out_refs = out_refs[-1], out_refs[:-1]
-        cotangents(capacity, owners, replicas, *sources[:4], sources[4:], cots_ref)
+        work_out = cotangents(capacity, owners, replicas, *sources[:4], sources[4:], cots_ref)
+        work_out(vols[0])
+        waiting = [vol for vol in range(held) if vol != vols[0]]
+    else:
+        waiting = []
     hidden = w2_ref.shape[1]
-    features = enc_t_ref.shape[1]
+    features = prepared[0][4].shape[0]
     samples = 8
     width = owners * capacity
     block = hidden // replicas
@@ -433,10 +447,10 @@
     hiddens, ins, heads = [], [], []
     for at, (n, vol, i) in enumerate(order):
         rows = slice(i * width, (i + CHUNK) * width)
-        act_two_ref, slope_one_ref, slope_two_ref, act_t_ref = prepared[n]
+        act_two_ref, slope_one_ref, slope_two_ref, act_t_ref, enc_t_ref = prepared[n]
         slope_one, slope_two = slope_one_ref[rows, :], slope_two_ref[rows, :]
         act_two = act_two_ref[rows, :]
-        act_t, enc_t, w2 = act_t_ref[:, rows], enc_t_ref[vol, :, rows], w2_ref[vol]
+        act_t, enc_t, w2 = act_t_ref[:, rows], enc_t_ref[:, rows], w2_ref[vol]
         cots = cots_ref[vol, :, rows].astype(BF)
         ahead = last(*order[at + 1]) if at + 1 < len(order) else None
         cot_two = pulled.astype(BF) * slope_two
@@ -449,6 +463,10 @@
             else:
                 total[n] = total[n] + part
         pulled = ahead
+        if waiting:
+            work_out(waiting.pop(0))
+    while waiting:
+        work_out(waiting.pop(0))
     for n in range(len(vols)):
         grad_hidden_s[n] = hiddens[n]
 
@@ -583,19 +601,18 @@
         half_in, ((0, 0), (features, 0), (hidden, 0))
     )
     half_hidden, half_head = late_hidden * half, late_head * half
-    w_head_t = lax.pad(
-        jnp.swapaxes(half_head, 1, 2),
-        jnp.zeros((), BF),
-        ((0, 0, 0), (0, 0, 0), (0, 127 - 3 * samples, samples - 1)),
+    w_head_t = jnp.pad(
+        jnp.repeat(jnp.swapaxes(half_head, 1, 2), samples, axis=2),
+        ((0, 0), (0, 0), (0, 128 - 4 * samples)),
     )
     w_head_8 = jnp.pad(half_head, ((0, 0), (0, 4), (0, 0)))
-    slots, enc_t, seg, gathering, terms, *stored = call(
+    slots, enc, seg, gathering, terms, *stored = call(
         functools.partial(forward_kernel, capacity),
         [VMEM] * 5,
         (arrived, selection(samples, zero), pair, half_hidden, w_head_t),
         (
             shape((held, PAYLOAD, width), F32),
-            shape((held, features, rows), BF),
+            shape((held, width, samples * features), BF),
             shape((held, 8, width), F32),
             shape((4 * owners, slot_width), F32),
             shape((held, 9 * samples, width), F32),
@@ -618,13 +635,14 @@
         late_slots = lax.optimization_barrier((slots, gathering))[0] if stage else slots
         outs = call(
             functools.partial(prepare_kernel, vols, order, slot_width),
-            [SMEM] + [VMEM] * (1 + 4 * len(vols)),
-            (where, late_slots) + tuple(stored[4 * vols[0] : 4 * vols[-1] + 4]),
+            [SMEM] + [VMEM] * (2 + 4 * len(vols)),
+            (where, late_slots, enc) + tuple(stored[4 * vols[0] : 4 * vols[-1] + 4]),
             (
                 shape((rows, hidden), BF),
                 shape((rows, hidden), BF),
                 shape((volume_count * capacity, width), BF),
                 shape((hidden, rows), BF),
+                shape((features, rows), BF),
             )
             * len(vols),
             flops=len(vols) * 3 * 10**9,
@@ -633,8 +651,8 @@
         *received, first_out = lax.optimization_barrier(tuple(received) + (outs[2],))
         outs = outs[:2] + (first_out,) + outs[3:]
         for n, vol in enumerate(vols):
-            slope_one, slope_two, hots[vol], act_t = outs[4 * n : 4 * n + 4]
-            prepared[vol] = (stored[4 * vol + 1], slope_one, slope_two, act_t)
+            slope_one, slope_two, hots[vol], act_t, enc_t = outs[5 * n : 5 * n + 5]
+            prepared[vol] = (stored[4 * vol + 1], slope_one, slope_two, act_t, enc_t)
         gathering = jnp.concatenate([gathering] + received, axis=0)
 
     block = hidden // replicas
@@ -647,8 +665,8 @@
             functools.partial(
                 backward_kernel, capacity, owners, replicas, vols, len(given) // 3, form
             ),
-            [SMEM] + [VMEM] * (3 + 4 * len(vols) + len(sources) + len(given)),
-            (where, half_hidden, w_head_8, enc_t)
+            [SMEM] + [VMEM] * (2 + 5 * len(vols) + len(sources) + len(given)),
+            (where, half_hidden, w_head_8)
             + sum((prepared[vol] for vol in vols), ())
             + sources
             + given,

time: 51.1 us -> 52.5 us (1.027)
  Pallas kernels: 21.3 us -> 22.8 us
    pallas_call x9, Pallas kernels: 21.3 us -> 22.8 us  [call(): pl.pallas_call(kernel, out_shape=out_shape, in_specs=list(specs), out_spe...]
    unnamed x12 -> x11, local copies, waits for them, and re-layouts: 1.55 us -> 1.88 us
  transfers between devices with their start and end apart: 10 -> 10, of which waited for: 4 -> 4; matrix products, arithmetic and copies ran while one was open for 2% -> 1% of each run, Pallas kernels for 19% -> 19%
where the time goes in v2:
time: 52.5 us; the launch traced here: 52.1 us
  Pallas kernels  22.8 us (43%)
  starting transfers between devices  18.5 us (35%)
  waiting for transfers between devices  7.37 us (14%)
  local copies, waits for them, and re-layouts  2.16 us (4%)
  between operations  0.9 us (2%)
    pallas_call x9, Pallas kernels, call(): pl.pallas_call(kernel, out_shape=out_shape, in_specs=list(specs), out_spe...  22.8 us
    all_to_all x1, starting transfers between devices, local(): lax.all_to_all(outgoing, 'vol', split_axis=0, concat_axis=0, tiled=True)  6.5 us
    ppermute x4, starting transfers between devices, local(): lax.ppermute(gathering, 'vol', [(at, at ^ n * stride) for at in range(own...  5.15 us
    all_to_all x1, waiting for transfers between devices, local(): lax.all_to_all(outgoing, 'vol', split_axis=0, concat_axis=0, tiled=True)  4.49 us
    ppermute x1, starting transfers between devices, local(): lax.ppermute(give, 'rep', [(at, at ^ 1) for at in range(replicas)])  3.8 us
    ppermute x3, waiting for transfers between devices, local(): pieces.append(lax.ppermute(outs[k], 'rep', steps(k, replicas)))  2.63 us
    unnamed x11, local copies, waits for them, and re-layouts  1.88 us
    ppermute x3, starting transfers between devices, local(): pieces.append(lax.ppermute(outs[k], 'rep', steps(k, replicas)))  1.7 us
  transfers between devices with their start and end apart: 10, of which 4 were waited for; matrix products, arithmetic and copies ran while one was open for 1% of the time, Pallas kernels for 19%

profile of v2, /device:TPU:1, one launch (start us, length us, event | category | flops | bytes accessed | tf_op | source)
XLA Modules:
  0.0 52.1 jit_solution(12466331758143052750)
XLA Ops:
  0.6 2.1 %shard_map.102 = (f32[8,40,128]{2,1,0:T(8,128)}, s32[1,512]{1,0:T(1,128)}) custom-call(f32[2,24,256]{2,1,0:T(8,128)} %bitcast.13, f32[2,8,256]{2,1,0:T(8,128)} %bitcast.14, s32[2,256]{1,0:T(2,128)} %bitcast.15, f32[3,256]{1,0:T(4,128)} %tgt_hbm.1), custom_call_target="tpu_custom_call" | custom-call | tf_op jit(solution)/shard_map/pallas_call | solution.py:540
  2.7 6.5 %all-to-all-start = ((f32[8,40,128]{2,1,0:T(8,128)}), f32[8,40,128]{2,1,0:T(8,128)S(1)}, u32[]{:S(2)}, u32[]{:S(2)}) async-start(f32[8,40,128]{2,1,0:T(8,128)} %get-tuple-element.83), calls=%async_computation | async-start | bytes 327680 | tf_op jit(solution)/shard_map/all_to_all | solution.py:597
  9.4 0.6 %copy-done.3 = bf16[4,4,256]{2,1,0:T(4,128)(2,1)S(1)} copy-done((bf16[4,4,256]{2,1,0:T(4,128)(2,1)S(1)}, bf16[4,4,256]{2,1,0:T(4,128)(2,1)}, u32[]{:S(2)}) %copy-start.3) | copy-done | bytes 8216
  10.6 0.5 %copy-done.1 = bf16[4,256,256]{2,1,0:T(8,128)(2,1)S(1)} copy-done((bf16[4,256,256]{2,1,0:T(8,128)(2,1)S(1)}, bf16[4,256,256]{2,1,0:T(8,128)(2,1)}, u32[]{:S(2)}) %copy-start.1) | copy-done | bytes 524312
  11.2 4.5 %all-to-all-done.in_ref = f32[8,40,128]{2,1,0:T(8,128)S(1)} async-done(((f32[8,40,128]{2,1,0:T(8,128)}), f32[8,40,128]{2,1,0:T(8,128)S(1)}, u32[]{:S(2)}, u32[]{:S(2)}) %all-to-all-start) | async-done | bytes 163872 | tf_op jit(solution)/shard_map/all_to_all | solution.py:597
  15.7 5.7 %shard_map.103 = (f32[4,40,256]{2,1,0:T(8,128)S(1)}, bf16[4,256,512]{2,1,0:T(8,128)(2,1)S(1)}, f32[4,8,256]{2,1,0:T(8,128)S(1)}, f32[32,128]{1,0:T(8,128)S(1)}, ...) custom-call(f32[8,40,128]{2,1,0:T(8,128)S(1)} %all-to-all-done.in_re, ...), custom_call_target="tpu_custom_call" | custom-call | flops 10000000000 | bytes 9765625 | tf_op jit(solution)/shard_map/pallas_call | solution.py:540
  21.4 1.5 %collective-permute-start.1 = (f32[32,128]{1,0:T(8,128)S(1)}, f32[32,128]{1,0:T(8,128)S(1)}, u32[]{:S(2)}, u32[]{:S(2)}) collective-permute-start(f32[32,128]{1,0:T(8,128)S(1)} %get-tuple-element.88), channel_id=1, source_target_pairs={{0,4},{1,5},{2,6},{3,7},{4,0},{5,1},{6,2},{7,3},{8,12},{9,13},{10,... | collective-permute-start | bytes 49160 | tf_op jit(solution)/shard_map/ppermute | solution.py:631
  22.9 2.0 %collective-permute-start.2 = (f32[32,128]{1,0:T(8,128)S(1)}, f32[32,128]{1,0:T(8,128)S(1)}, u32[]{:S(2)}, u32[]{:S(2)}) collective-permute-start(f32[32,128]{1,0:T(8,128)S(1)} %get-tuple-element.88), channel_id=1, source_target_pairs={{0,6},{1,7},{2,4},{3,5},{4,2},{5,3},{6,0},{7,1},{8,14},{9,15},{10,... | collective-permute-start | bytes 49160 | tf_op jit(solution)/shard_map/ppermute | solution.py:631
  25.0 2.1 %shard_map.104 = (bf16[2048,256]{1,0:T(8,128)(2,1)S(1)}, bf16[2048,256]{1,0:T(8,128)(2,1)S(1)}, bf16[1024,256]{1,0:T(8,128)(2,1)S(1)}, bf16[256,2048]{1,0:T(8,12...) custom-call(s32[2]{0:T(128)S(1)} %pad_add_fusion.1.refs_0_.where_ref, ...), custom_call_target="tpu_custom_call" | custom-call | flops 6000000000 | bytes 5859375 | tf_op jit(solution)/shard_map/pallas_call | solution.py:540
  27.1 0.2 collective-permute-done.2
  27.3 1.6 %collective-permute-start.3 = (f32[128,128]{1,0:T(8,128)S(1)}, f32[128,128]{1,0:T(8,128)S(1)}, u32[]{:S(2)}, u32[]{:S(2)}) collective-permute-start(f32[128,128]{1,0:T(8,128)S(1)} %get-tuple-element.158), channel_id=1, source_target_pairs={{0,1},{1,0},{2,3},{3,2},{4,5},{5,4},{6,7},{7,6},{8,9},{9,8},{10,11... | collective-permute-start | bytes 196616 | tf_op jit(solution)/shard_map/ppermute | solution.py:631
  28.9 2.1 %shard_map.105 = (bf16[2048,256]{1,0:T(8,128)(2,1)S(1)}, bf16[2048,256]{1,0:T(8,128)(2,1)S(1)}, bf16[1024,256]{1,0:T(8,128)(2,1)S(1)}, bf16[256,2048]{1,0:T(8,12...) custom-call(s32[2]{0:T(128)S(1)} %pad_add_fusion.1.refs_0_.where_ref, ...), custom_call_target="tpu_custom_call" | custom-call | flops 6000000000 | bytes 5859375 | tf_op jit(solution)/shard_map/pallas_call | solution.py:540
  31.0 4.5 %shard_map.106 = (bf16[2,176,256]{2,1,0:T(8,128)(2,1)S(1)}, bf16[2,176,256]{2,1,0:T(8,128)(2,1)S(1)}, f32[4,8,2048]{2,1,0:T(8,128)S(1)}) custom-call(s32[2]{0:T(128)S(1)} %pad_add_fusion.1.refs_0_.where_ref, bf16[4,256,256]{2,1,0:T(8,128)(2,1)S(1)} %broadcast_multiply_fusion.w2_ref.refs_1_, bf16[4,8,256]{2,1,0:T(8,128)(2,1)S(1)} %pad.19.refs_2_, ...), custom_call_target="tpu_custom_call" | custom-call | flops 10000000000 | bytes 9765625 | tf_op jit(solution)/shard_map/pallas_call | solution.py:540
  35.5 3.8 %collective-permute-start.4 = (bf16[2,176,256]{2,1,0:T(8,128)(2,1)S(1)}, bf16[2,176,256]{2,1,0:T(8,128)(2,1)S(1)}, u32[]{:S(2)}, u32[]{:S(2)}) collective-permute-start(bf16[2,176,256]{2,1,0:T(8,128)(2,1)S(1)} %get-tuple-element.133), channel_id=1, source_target_pairs={{0,8},{8,0},{16,24},{24,16},{1,9},{9,1},{17,25},{25,17},{2,10},{10... | collective-permute-start | bytes 540680 | tf_op jit(solution)/shard_map/ppermute | solution.py:686
  39.3 1.9 %shard_map.107 = (f32[256,256]{1,0:T(8,128)S(1)}, f32[64,256]{1,0:T(8,128)S(1)}, f32[8,256]{1,0:T(8,128)S(1)}) custom-call(s32[2]{0:T(128)S(1)} %pad_add_fusion.1.refs_0_.where_ref, bf16[4,256,256]{2,1,0:T(8,128)(2,1)S(1)} %broadcast_multiply_fusion.w2_ref.refs_1_, bf16[4,8,256]{2,1,0:T(8,128)(2,1)S(1)} %pad.19.refs_2_, ...), custom_call_target="tpu_custom_call" | custom-call | flops 5000000000 | bytes 4882812 | tf_op jit(solution)/shard_map/pallas_call | solution.py:540
  41.4 1.3 %collective-permute-start.5 = (bf16[176,256]{1,0:T(8,128)(2,1)S(1)}, bf16[176,256]{1,0:T(8,128)(2,1)S(1)}, u32[]{:S(2)}, u32[]{:S(2)}) collective-permute-start(bf16[176,256]{1,0:T(8,128)(2,1)S(1)} %fusion.22), channel_id=1, source_target_pairs={{0,16},{8,24},{16,0},{24,8},{1,17},{9,25},{17,1},{25,9},{2,18},{10... | collective-permute-start | bytes 270344 | tf_op jit(solution)/shard_map/ppermute | solution.py:705
  42.7 2.1 %shard_map.108 = (bf16[176,256]{1,0:T(8,128)(2,1)S(1)}, bf16[176,256]{1,0:T(8,128)(2,1)S(1)}, bf16[176,256]{1,0:T(8,128)(2,1)S(1)}, bf16[176,256]{1,0:T(8,128)(2,1)S(1)}) custom-call(s32[2]{0:T(128)S(1)} %pad_add_fusion.1.refs_0_.where_ref, bf16[4,256,256]{2,1,0:T(8,128)(2,1)S(1)} %broadcast_multiply_fusion.w2_ref.refs_1_, ...), custom_call_target="tpu_custom_call" | custom-call | flops 5000000000 | bytes 4882812 | tf_op jit(solution)/shard_map/pallas_call | solution.py:540
  44.8 0.5 collective-permute-start.6
  45.3 1.2 %collective-permute-start.7 = (bf16[176,256]{1,0:T(8,128)(2,1)S(1)}, bf16[176,256]{1,0:T(8,128)(2,1)S(1)}, u32[]{:S(2)}, u32[]{:S(2)}) collective-permute-start(bf16[176,256]{1,0:T(8,128)(2,1)S(1)} %get-tuple-element.153), channel_id=1, source_target_pairs={{0,16},{8,24},{16,0},{24,8},{1,17},{9,25},{17,1},{25,9},{2,18},{10... | collective-permute-start | bytes 270344 | tf_op jit(solution)/shard_map/ppermute | solution.py:713
  46.5 0.7 %copy-done = s32[1,512]{1,0:T(1,128)S(1)} copy-done((s32[1,512]{1,0:T(1,128)S(1)}, s32[1,512]{1,0:T(1,128)}, u32[]{:S(2)}) %copy-start) | copy-done | bytes 2072
  47.2 1.5 %shard_map.109 = f32[3,256]{1,0:T(4,128)} custom-call(s32[2]{0:T(128)S(1)} %pad_add_fusion.1.refs_0_.where_ref, s32[1,512]{1,0:T(1,128)S(1)} %copy-done, f32[256,128]{1,0:T(8,128)S(1)} %constant_dynamic-update-slice_fusion.4.refs_13_.all_ref), custom_call_target="tpu_custom_call" | custom-call | tf_op jit(solution)/shard_map/pallas_call | solution.py:540
  48.7 1.9 %collective-permute-done.7.refs_4_ = bf16[176,256]{1,0:T(8,128)(2,1)S(1)} collective-permute-done((bf16[176,256]{1,0:T(8,128)(2,1)S(1)}, bf16[176,256]{1,0:T(8,128)(2,1)S(1)}, u32[]{:S(2)}, u32[]{:S(2)}) %collective-permute-start.7) | collective-permute-done | bytes 90144 | tf_op jit(solution)/shard_map/ppermute | solution.py:713
  50.5 0.8 %collective-permute-done.8.refs_5_ = bf16[176,256]{1,0:T(8,128)(2,1)S(1)} collective-permute-done((bf16[176,256]{1,0:T(8,128)(2,1)S(1)}, bf16[176,256]{1,0:T(8,128)(2,1)S(1)}, u32[]{:S(2)}, u32[]{:S(2)}) %collective-permute-start.8) | collective-permute-done | bytes 90144 | tf_op jit(solution)/shard_map/ppermute | solution.py:713
  51.3 0.8 %shard_map.110 = (f32[4,64,64]{2,1,0:T(8,128)}, f32[4,64,256]{2,1,0:T(8,128)}, f32[4,4,64]{2,1,0:T(4,128)}) custom-call(f32[176,256]{1,0:T(8,128)S(1)} %slice_bitcast_fusion.refs_0_, bf16[176,256]{1,0:T(8,128)(2,1)S(1)} %collective-permute-done.5.refs_1_, bf16[176,256]{1,0:T(8,128)(2,1)S(1)} %get-tuple-element.150.refs_2_, ...), custom_call_target="tpu_custom_call" | custom-call | tf_op jit(solution)/shard_map/pallas_call | solution.py:540
  (37 shorter events, 0.8 us)
Async XLA Ops:
  2.7 6.6 %copy-start.2 = (bf16[4,64,256]{2,1,0:T(8,128)(2,1)S(1)}, bf16[4,64,256]{2,1,0:T(8,128)(2,1)}, u32[]{:S(2)}) copy-start(bf16[4,64,256]{2,1,0:T(8,128)(2,1)} %param.11) | copy-start | bytes 393220
  2.7 12.9 %all-to-all-start = ((f32[8,40,128]{2,1,0:T(8,128)}), f32[8,40,128]{2,1,0:T(8,128)S(1)}, u32[]{:S(2)}, u32[]{:S(2)}) async-start(f32[8,40,128]{2,1,0:T(8,128)} %get-tuple-element.83), calls=%async_computation | async-start | bytes 327680 | tf_op jit(solution)/shard_map/all_to_all | solution.py:597
  9.3 0.7 %copy-start.3 = (bf16[4,4,256]{2,1,0:T(4,128)(2,1)S(1)}, bf16[4,4,256]{2,1,0:T(4,128)(2,1)}, u32[]{:S(2)}) copy-start(bf16[4,4,256]{2,1,0:T(4,128)(2,1)} %param.13) | copy-start | bytes 24580
  10.1 1.0 %copy-start.1 = (bf16[4,256,256]{2,1,0:T(8,128)(2,1)S(1)}, bf16[4,256,256]{2,1,0:T(8,128)(2,1)}, u32[]{:S(2)}) copy-start(bf16[4,256,256]{2,1,0:T(8,128)(2,1)} %param.12) | copy-start | bytes 1572868
  21.4 5.7 %collective-permute-start = (f32[32,128]{1,0:T(8,128)S(1)}, f32[32,128]{1,0:T(8,128)S(1)}, u32[]{:S(2)}, u32[]{:S(2)}) collective-permute-start(f32[32,128]{1,0:T(8,128)S(1)} %get-tuple-element.88), channel_id=1, source_target_pairs={{0,2},{1,3},{2,0},{3,1},{4,6},{5,7},{6,4},{7,5},{8,10},{9,11},{10,... | collective-permute-start | bytes 49160 | tf_op jit(solution)/shard_map/ppermute | solution.py:631
  21.4 5.7 %collective-permute-start.1 = (f32[32,128]{1,0:T(8,128)S(1)}, f32[32,128]{1,0:T(8,128)S(1)}, u32[]{:S(2)}, u32[]{:S(2)}) collective-permute-start(f32[32,128]{1,0:T(8,128)S(1)} %get-tuple-element.88), channel_id=1, source_target_pairs={{0,4},{1,5},{2,6},{3,7},{4,0},{5,1},{6,2},{7,3},{8,12},{9,13},{10,... | collective-permute-start | bytes 49160 | tf_op jit(solution)/shard_map/ppermute | solution.py:631
  22.9 4.4 %collective-permute-start.2 = (f32[32,128]{1,0:T(8,128)S(1)}, f32[32,128]{1,0:T(8,128)S(1)}, u32[]{:S(2)}, u32[]{:S(2)}) collective-permute-start(f32[32,128]{1,0:T(8,128)S(1)} %get-tuple-element.88), channel_id=1, source_target_pairs={{0,6},{1,7},{2,4},{3,5},{4,2},{5,3},{6,0},{7,1},{8,14},{9,15},{10,... | collective-permute-start | bytes 49160 | tf_op jit(solution)/shard_map/ppermute | solution.py:631
  27.3 3.7 %collective-permute-start.3 = (f32[128,128]{1,0:T(8,128)S(1)}, f32[128,128]{1,0:T(8,128)S(1)}, u32[]{:S(2)}, u32[]{:S(2)}) collective-permute-start(f32[128,128]{1,0:T(8,128)S(1)} %get-tuple-element.158), channel_id=1, source_target_pairs={{0,1},{1,0},{2,3},{3,2},{4,5},{5,4},{6,7},{7,6},{8,9},{9,8},{10,11... | collective-permute-start | bytes 196616 | tf_op jit(solution)/shard_map/ppermute | solution.py:631
  35.5 5.8 %collective-permute-start.4 = (bf16[2,176,256]{2,1,0:T(8,128)(2,1)S(1)}, bf16[2,176,256]{2,1,0:T(8,128)(2,1)S(1)}, u32[]{:S(2)}, u32[]{:S(2)}) collective-permute-start(bf16[2,176,256]{2,1,0:T(8,128)(2,1)S(1)} %get-tuple-element.133), channel_id=1, source_target_pairs={{0,8},{8,0},{16,24},{24,16},{1,9},{9,1},{17,25},{25,17},{2,10},{10... | collective-permute-start | bytes 540680 | tf_op jit(solution)/shard_map/ppermute | solution.py:686
  41.4 7.3 %collective-permute-start.5 = (bf16[176,256]{1,0:T(8,128)(2,1)S(1)}, bf16[176,256]{1,0:T(8,128)(2,1)S(1)}, u32[]{:S(2)}, u32[]{:S(2)}) collective-permute-start(bf16[176,256]{1,0:T(8,128)(2,1)S(1)} %fusion.22), channel_id=1, source_target_pairs={{0,16},{8,24},{16,0},{24,8},{1,17},{9,25},{17,1},{25,9},{2,18},{10... | collective-permute-start | bytes 270344 | tf_op jit(solution)/shard_map/ppermute | solution.py:705
  44.8 3.9 %collective-permute-start.6 = (bf16[176,256]{1,0:T(8,128)(2,1)S(1)}, bf16[176,256]{1,0:T(8,128)(2,1)S(1)}, u32[]{:S(2)}, u32[]{:S(2)}) collective-permute-start(bf16[176,256]{1,0:T(8,128)(2,1)S(1)} %get-tuple-element.152), channel_id=1, source_target_pairs={{0,8},{8,16},{16,24},{24,0},{1,9},{9,17},{17,25},{25,1},{2,10},{10... | collective-permute-start | bytes 270344 | tf_op jit(solution)/shard_map/ppermute | solution.py:713
  45.3 5.3 %collective-permute-start.7 = (bf16[176,256]{1,0:T(8,128)(2,1)S(1)}, bf16[176,256]{1,0:T(8,128)(2,1)S(1)}, u32[]{:S(2)}, u32[]{:S(2)}) collective-permute-start(bf16[176,256]{1,0:T(8,128)(2,1)S(1)} %get-tuple-element.153), channel_id=1, source_target_pairs={{0,16},{8,24},{16,0},{24,8},{1,17},{9,25},{17,1},{25,9},{2,18},{10... | collective-permute-start | bytes 270344 | tf_op jit(solution)/shard_map/ppermute | solution.py:713
  46.5 4.8 %collective-permute-start.8 = (bf16[176,256]{1,0:T(8,128)(2,1)S(1)}, bf16[176,256]{1,0:T(8,128)(2,1)S(1)}, u32[]{:S(2)}, u32[]{:S(2)}) collective-permute-start(bf16[176,256]{1,0:T(8,128)(2,1)S(1)} %get-tuple-element.154), channel_id=1, source_target_pairs={{0,24},{8,0},{16,8},{24,16},{1,25},{9,1},{17,9},{25,17},{2,26},{10... | collective-permute-start | bytes 270344 | tf_op jit(solution)/shard_map/ppermute | solution.py:713
  46.5 0.7 %copy-start = (s32[1,512]{1,0:T(1,128)S(1)}, s32[1,512]{1,0:T(1,128)}, u32[]{:S(2)}) copy-start(s32[1,512]{1,0:T(1,128)} %get-tuple-element.81.place_ref) | copy-start | bytes 6148
